TPU v7x, 512 devices: a whole 4x4x16 slice. The times are simulated.
512 devices in a mesh: dom: 64 (over y_lo, z, core), orb: 8 (over y_hi, x).
Axes of the slice: x: 4, y: 4 (y_hi: 2, y_lo: 2; y = y_hi * 2 + y_lo), z: 16, core: 2. Of those that a mesh axis runs over, the one named last changes fastest.
Arguments:
- orbitals: float32 [96, 64, 6, 8, 128], P('orb', 'dom'), may hold values from -6 to 6
- potential: float32 [64, 6, 8, 128], P('dom'), may hold values from 0.1 to 1.5
Outputs:
- rotated: float32 [96, 64, 6, 8, 128], P('orb', 'dom')
- subspace_h: float32 [96, 96], replicated
All inputs are finite; a program needn't handle non-finite values.
Results may differ from a plain program's by a relative error of at most 0.000071.
Values sent between devices are 32-bit elements; how exact they have to be, the bound alone decides.
A program may use at most 64 MiB of HBM per device.

v0:
```python
import jax
import jax.numpy as jnp
from jax import lax
from jax.sharding import PartitionSpec as P

DEGREE = 8
RADIUS = 6
PCOLS = 8


COEF = (
    -5369.0 / 1800.0,
    12.0 / 7.0,
    -15.0 / 56.0,
    10.0 / 189.0,
    -1.0 / 112.0,
    2.0 / 1925.0,
    -1.0 / 16632.0,
)
E_HALF = 6.0
CENTER = 8.0
A_LOW = 0.0


def from_behind(value, axis, steps):
    count = lax.axis_size(axis)
    initial, last = (max(0, -steps), min(count, count - steps))
    return lax.ppermute(value, axis, [(source, source + steps) for source in range(initial, last)])


def hamiltonian(field, pot, keep_low, keep_high):
    rad = RADIUS
    nx = field.shape[1]
    ny = field.shape[2]
    nz = field.shape[3]
    row_parts = []
    for sign in (1, -1):
        rim = field if sign == 1 else field
        row_parts.append(from_behind(rim, "dom", sign * PCOLS))
    col_parts = []
    for sign in (1, -1):
        rim = field[:, :, ny - rad :] if sign == 1 else field[:, :, :rad]
        col_parts.append(from_behind(rim, "dom", sign))
    row_ext = jnp.concatenate([row_parts[0], field, row_parts[1]], axis=1)
    col_ext = jnp.concatenate([col_parts[0] * keep_low, field, col_parts[1] * keep_high], axis=2)
    z_ext = jnp.pad(field, ((0, 0), (0, 0), (0, 0), (rad, rad)))
    lap = 3.0 * COEF[0] * field
    for k in range(1, rad + 1):
        term = row_ext[:, rad + k : rad + k + nx] + row_ext[:, rad - k : rad - k + nx]
        term = term + col_ext[:, :, rad + k : rad + k + ny] + col_ext[:, :, rad - k : rad - k + ny]
        term = (
            term + z_ext[:, :, :, rad + k : rad + k + nz] + z_ext[:, :, :, rad - k : rad - k + nz]
        )
        lap = lap + COEF[k] * term
    return -0.5 * lap + pot * field


def local(orbitals, potential):
    hi = lax.Precision.HIGHEST
    local_orb = orbitals.shape[0]
    nx = orbitals.shape[2]
    ny = orbitals.shape[3]
    nz = orbitals.shape[4]
    field = orbitals[:, 0]
    pot = potential[0]
    column = lax.axis_index("dom") % PCOLS
    keep_low = (column != 0).astype(jnp.float32)
    keep_high = (column != PCOLS - 1).astype(jnp.float32)
    sigma = E_HALF / (A_LOW - CENTER)
    sigma_one = sigma
    older = field
    newer = (hamiltonian(older, pot, keep_low, keep_high) - CENTER * older) * (sigma_one / E_HALF)
    for step in range(2, DEGREE + 1):
        sigma_next = 1.0 / (2.0 / sigma_one - sigma)
        latest = (hamiltonian(newer, pot, keep_low, keep_high) - CENTER * newer) * (
            2.0 * sigma_next / E_HALF
        ) - sigma * sigma_next * older
        older = newer
        newer = latest
        sigma = sigma_next
    applied = hamiltonian(newer, pot, keep_low, keep_high)
    cells = nx * ny * nz
    flat_f = newer.reshape(local_orb, cells)
    flat_a = applied.reshape(local_orb, cells)
    norb = local_orb * lax.axis_size("orb")
    total_cells = float(cells * lax.axis_size("dom"))
    first = lax.axis_index("orb") * local_orb
    piece = lax.all_gather(flat_f, "orb", axis=0, tiled=True)
    over_rows = jnp.dot(piece, flat_f.T, precision=hi)
    proj_rows = jnp.dot(piece, flat_a.T, precision=hi)
    blank = jnp.zeros((norb, norb), jnp.float32)
    over_part = lax.dynamic_update_slice(blank, over_rows, (0, first))
    proj_part = lax.dynamic_update_slice(blank, proj_rows, (0, first))
    over_sum, proj_sum = lax.psum((over_part, proj_part), ("dom", "orb"))
    intersection = over_sum / total_cells
    projected = proj_sum / total_cells
    lower = jnp.linalg.cholesky(intersection)
    inverse = lax.linalg.triangular_solve(
        lower, jnp.eye(norb, dtype=jnp.float32), left_side=True, lower=True
    )
    subspace_h = jnp.dot(jnp.dot(inverse, projected, precision=hi), inverse.T, precision=hi)
    my_rows = lax.dynamic_slice_in_dim(inverse, first, local_orb, 0)
    rotated = jnp.dot(my_rows, lax.all_gather(flat_f, "orb", axis=0, tiled=True), precision=hi)
    return (rotated.reshape(local_orb, 1, nx, ny, nz), subspace_h)


def solution(mesh):
    return jax.shard_map(
        local,
        mesh=mesh,
        in_specs=(P("orb", "dom", None, None, None), P("dom", None, None, None)),
        out_specs=(P("orb", "dom", None, None, None), P()),
        check_vma=False,
    )
```

profile of v0, /device:TPU:1, one launch (start us, length us, event | category | flops | bytes accessed | tf_op | source)
XLA Modules:
  0.0 910.9 jit_solution(6478088178720368656)
XLA Ops:
  14.6 9.5 %collective-permute-start.1 = (f32[12,6,8,128]{3,2,1,0:T(8,128)}, f32[12,6,8,128]{3,2,1,0:T(8,128)S(1)}, u32[]{:S(2)}, u32[]{:S(2)}) collective-permute-start(f32[12,6,8,128]{3,2,1,0:T(8,128)} %bitcast.43), channel_id=1, source_target_pairs={{0,64},{8,72},{16,80},{24,88},{32,96},{40,104},{48,112},{56,120},{... | collective-permute-start | bytes 884744 | tf_op jit(solution)/shard_map/ppermute | solution.py:28
  32.9 15.9 %collective-permute-done = f32[12,6,8,128]{3,2,1,0:T(8,128)S(1)} collective-permute-done((f32[12,6,8,128]{3,2,1,0:T(8,128)}, f32[12,6,8,128]{3,2,1,0:T(8,128)S(1)}, u32[]{:S(2)}, u32[]{:S(2)}) %collective-permute-start) | collective-permute-done | bytes 294944 | tf_op jit(solution)/shard_map/ppermute | solution.py:28
  52.1 8.4 collective-permute-start.5
  64.5 6.1 collective-permute-done.6
  70.6 25.1 %collective-permute-done.4 = f32[12,6,8,128]{3,2,1,0:T(8,128)S(1)} collective-permute-done((f32[12,6,8,128]{3,2,1,0:T(8,128)S(1)}, f32[12,6,8,128]{3,2,1,0:T(8,128)S(1)}, u32[]{:S(2)}, u32[]{:S(2)}) %collective-permute-start.4) | collective-permute-done | bytes 294944 | tf_op jit(solution)/shard_map/ppermute | solution.py:28
  99.1 7.5 collective-permute-start.9
  110.6 6.2 collective-permute-done.10
  116.9 7.2 collective-permute-done.9
  124.1 9.0 collective-permute-done.8
  136.4 12.1 %collective-permute-start.13 = (f32[12,6,8,128]{3,2,1,0:T(8,128)S(1)}, f32[12,6,8,128]{3,2,1,0:T(8,128)S(1)}, u32[]{:S(2)}, u32[]{:S(2)}) collective-permute-start(f32[12,6,8,128]{3,2,1,0:T(8,128)S(1)} %fusion.270), channel_id=1, source_target_pairs={{0,64},{8,72},{16,80},{24,88},{32,96},{40,104},{48,112},{56,120},{... | collective-permute-start | bytes 884744 | tf_op jit(solution)/shard_map/ppermute | solution.py:28
  152.7 11.0 %collective-permute-done.14 = f32[12,6,6,128]{3,2,1,0:T(8,128)S(1)} collective-permute-done((f32[12,6,6,128]{3,2,1,0:T(8,128)S(1)}, f32[12,6,6,128]{3,2,1,0:T(8,128)S(1)}, u32[]{:S(2)}, u32[]{:S(2)}) %collective-permute-start.14) | collective-permute-done | bytes 221216 | tf_op jit(solution)/shard_map/ppermute | solution.py:28
  165.2 19.1 %collective-permute-start.19 = (f32[12,6,6,128]{3,2,1,0:T(8,128)S(1)}, f32[12,6,6,128]{3,2,1,0:T(8,128)S(1)}, u32[]{:S(2)}, u32[]{:S(2)}) collective-permute-start(f32[12,6,6,128]{3,2,1,0:T(8,128)S(1)} %get-tuple-element.21), channel_id=1, source_target_pairs={{0,8},{8,16},{16,24},{24,32},{32,40},{40,48},{48,56},{56,64},{64,7... | collective-permute-start | bytes 663560 | tf_op jit(solution)/shard_map/ppermute | solution.py:28
  184.3 10.3 %collective-permute-start.17 = (f32[12,6,8,128]{3,2,1,0:T(8,128)S(1)}, f32[12,6,8,128]{3,2,1,0:T(8,128)S(1)}, u32[]{:S(2)}, u32[]{:S(2)}) collective-permute-start(f32[12,6,8,128]{3,2,1,0:T(8,128)S(1)} %fusion.227), channel_id=1, source_target_pairs={{0,64},{8,72},{16,80},{24,88},{32,96},{40,104},{48,112},{56,120},{... | collective-permute-start | bytes 884744 | tf_op jit(solution)/shard_map/ppermute | solution.py:28
  197.9 6.5 collective-permute-done.18
  204.4 13.2 %collective-permute-done.17 = f32[12,6,8,128]{3,2,1,0:T(8,128)S(1)} collective-permute-done((f32[12,6,8,128]{3,2,1,0:T(8,128)S(1)}, f32[12,6,8,128]{3,2,1,0:T(8,128)S(1)}, u32[]{:S(2)}, u32[]{:S(2)}) %collective-permute-start.17) | collective-permute-done | bytes 294944 | tf_op jit(solution)/shard_map/ppermute | solution.py:28
  217.6 10.2 %collective-permute-done.16 = f32[12,6,8,128]{3,2,1,0:T(8,128)S(1)} collective-permute-done((f32[12,6,8,128]{3,2,1,0:T(8,128)S(1)}, f32[12,6,8,128]{3,2,1,0:T(8,128)S(1)}, u32[]{:S(2)}, u32[]{:S(2)}) %collective-permute-start.16) | collective-permute-done | bytes 294944 | tf_op jit(solution)/shard_map/ppermute | solution.py:28
  231.2 5.2 collective-permute-start.21
  240.4 5.4 collective-permute-done.22
  249.9 20.2 %collective-permute-done.20 = f32[12,6,8,128]{3,2,1,0:T(8,128)S(1)} collective-permute-done((f32[12,6,8,128]{3,2,1,0:T(8,128)S(1)}, f32[12,6,8,128]{3,2,1,0:T(8,128)S(1)}, u32[]{:S(2)}, u32[]{:S(2)}) %collective-permute-start.20) | collective-permute-done | bytes 294944 | tf_op jit(solution)/shard_map/ppermute | solution.py:28
  273.4 5.2 collective-permute-start.25
  282.7 5.6 collective-permute-done.26
  288.7 23.4 %collective-permute-done.24 = f32[12,6,8,128]{3,2,1,0:T(8,128)S(1)} collective-permute-done((f32[12,6,8,128]{3,2,1,0:T(8,128)S(1)}, f32[12,6,8,128]{3,2,1,0:T(8,128)S(1)}, u32[]{:S(2)}, u32[]{:S(2)}) %collective-permute-start.24) | collective-permute-done | bytes 294944 | tf_op jit(solution)/shard_map/ppermute | solution.py:28
  315.5 5.7 collective-permute-start.29
  325.2 9.9 %collective-permute-done.30 = f32[12,6,6,128]{3,2,1,0:T(8,128)S(1)} collective-permute-done((f32[12,6,6,128]{3,2,1,0:T(8,128)S(1)}, f32[12,6,6,128]{3,2,1,0:T(8,128)S(1)}, u32[]{:S(2)}, u32[]{:S(2)}) %collective-permute-start.30) | collective-permute-done | bytes 221216 | tf_op jit(solution)/shard_map/ppermute | solution.py:28
  335.2 18.5 %collective-permute-done.28 = f32[12,6,8,128]{3,2,1,0:T(8,128)S(1)} collective-permute-done((f32[12,6,8,128]{3,2,1,0:T(8,128)S(1)}, f32[12,6,8,128]{3,2,1,0:T(8,128)S(1)}, u32[]{:S(2)}, u32[]{:S(2)}) %collective-permute-start.28) | collective-permute-done | bytes 294944 | tf_op jit(solution)/shard_map/ppermute | solution.py:28
  357.9 8.4 collective-permute-start.33
  370.7 5.8 collective-permute-done.34
  379.1 20.6 %collective-permute-done.32 = f32[12,6,8,128]{3,2,1,0:T(8,128)S(1)} collective-permute-done((f32[12,6,8,128]{3,2,1,0:T(8,128)S(1)}, f32[12,6,8,128]{3,2,1,0:T(8,128)S(1)}, u32[]{:S(2)}, u32[]{:S(2)}) %collective-permute-start.32) | collective-permute-done | bytes 294944 | tf_op jit(solution)/shard_map/ppermute | solution.py:28
  401.1 31.5 %all-gather.3.cloned.1.call-done = f32[8,12,6144]{2,1,0:T(8,128)} async-done(((f32[1,12,6144]{2,1,0:T(8,128)}), f32[8,12,6144]{2,1,0:T(8,128)}) %all-gather.3.cloned.1.call-update) | async-done | bytes 2359312 | tf_op jit(solution)/shard_map/all_gather | solution.py:88
  440.0 441.6 %all-reduce.12.cloned.1.call-done = (f32[96,96]{1,0:T(8,128)}, f32[96,96]{1,0:T(8,128)}) async-done(((f32[96,96]{1,0:T(8,128)}, f32[96,96]{1,0:T(8,128)}), (f32[96,96]{1,0:T(8,128)}, f32[96,96]{1,0:T(8,128)})) %all-reduce.12.cloned.1.call-update) | async-done | bytes 73744 | tf_op jit(solution)/shard_map/psum | solution.py:94
  883.3 8.8 cholesky.16
  893.4 7.4 custom-call.6
  (119 shorter events, 95.4 us)
Async XLA Ops:
  7.2 425.4 %all-gather.3.cloned.1.call-start = ((), (), s32[]{:S(2)}) async-start(), calls=%async_computation | async-start | bytes 3538944 | tf_op jit(solution)/shard_map/all_gather | solution.py:88
  8.4 19.9 %collective-permute-start.3 = (f32[12,6,6,128]{3,2,1,0:T(8,128)S(1)}, f32[12,6,6,128]{3,2,1,0:T(8,128)S(1)}, u32[]{:S(2)}, u32[]{:S(2)}) collective-permute-start(f32[12,6,6,128]{3,2,1,0:T(8,128)S(1)} %get-tuple-element.29), channel_id=1, source_target_pairs={{0,8},{8,16},{16,24},{24,32},{32,40},{40,48},{48,56},{56,64},{64,7... | collective-permute-start | bytes 663560 | tf_op jit(solution)/shard_map/ppermute | solution.py:28
  13.3 35.4 %collective-permute-start = (f32[12,6,8,128]{3,2,1,0:T(8,128)}, f32[12,6,8,128]{3,2,1,0:T(8,128)S(1)}, u32[]{:S(2)}, u32[]{:S(2)}) collective-permute-start(f32[12,6,8,128]{3,2,1,0:T(8,128)} %bitcast.42), channel_id=1, source_target_pairs={{64,0},{72,8},{80,16},{88,24},{96,32},{104,40},{112,48},{120,56},{... | collective-permute-start | bytes 884744 | tf_op jit(solution)/shard_map/ppermute | solution.py:28
  14.6 34.1 %collective-permute-start.1 = (f32[12,6,8,128]{3,2,1,0:T(8,128)}, f32[12,6,8,128]{3,2,1,0:T(8,128)S(1)}, u32[]{:S(2)}, u32[]{:S(2)}) collective-permute-start(f32[12,6,8,128]{3,2,1,0:T(8,128)} %bitcast.43), channel_id=1, source_target_pairs={{0,64},{8,72},{16,80},{24,88},{32,96},{40,104},{48,112},{56,120},{... | collective-permute-start | bytes 884744 | tf_op jit(solution)/shard_map/ppermute | solution.py:28
  50.1 14.4 %collective-permute-start.7 = (f32[12,6,6,128]{3,2,1,0:T(8,128)S(1)}, f32[12,6,6,128]{3,2,1,0:T(8,128)S(1)}, u32[]{:S(2)}, u32[]{:S(2)}) collective-permute-start(f32[12,6,6,128]{3,2,1,0:T(8,128)S(1)} %get-tuple-element.27), channel_id=1, source_target_pairs={{0,8},{8,16},{16,24},{24,32},{32,40},{40,48},{48,56},{56,64},{64,7... | collective-permute-start | bytes 663560 | tf_op jit(solution)/shard_map/ppermute | solution.py:28
  52.1 18.5 %collective-permute-start.5 = (f32[12,6,8,128]{3,2,1,0:T(8,128)S(1)}, f32[12,6,8,128]{3,2,1,0:T(8,128)S(1)}, u32[]{:S(2)}, u32[]{:S(2)}) collective-permute-start(f32[12,6,8,128]{3,2,1,0:T(8,128)S(1)} %get-tuple-element.10), channel_id=1, source_target_pairs={{0,64},{8,72},{16,80},{24,88},{32,96},{40,104},{48,112},{56,120},{... | collective-permute-start | bytes 884744 | tf_op jit(solution)/shard_map/ppermute | solution.py:28
  60.5 35.2 %collective-permute-start.4 = (f32[12,6,8,128]{3,2,1,0:T(8,128)S(1)}, f32[12,6,8,128]{3,2,1,0:T(8,128)S(1)}, u32[]{:S(2)}, u32[]{:S(2)}) collective-permute-start(f32[12,6,8,128]{3,2,1,0:T(8,128)S(1)} %get-tuple-element.10), channel_id=1, source_target_pairs={{64,0},{72,8},{80,16},{88,24},{96,32},{104,40},{112,48},{120,56},{... | collective-permute-start | bytes 884744 | tf_op jit(solution)/shard_map/ppermute | solution.py:28
  97.1 13.4 %collective-permute-start.11 = (f32[12,6,6,128]{3,2,1,0:T(8,128)S(1)}, f32[12,6,6,128]{3,2,1,0:T(8,128)S(1)}, u32[]{:S(2)}, u32[]{:S(2)}) collective-permute-start(f32[12,6,6,128]{3,2,1,0:T(8,128)S(1)} %get-tuple-element.25), channel_id=1, source_target_pairs={{0,8},{8,16},{16,24},{24,32},{32,40},{40,48},{48,56},{56,64},{64,7... | collective-permute-start | bytes 663560 | tf_op jit(solution)/shard_map/ppermute | solution.py:28
  99.1 25.0 %collective-permute-start.9 = (f32[12,6,8,128]{3,2,1,0:T(8,128)S(1)}, f32[12,6,8,128]{3,2,1,0:T(8,128)S(1)}, u32[]{:S(2)}, u32[]{:S(2)}) collective-permute-start(f32[12,6,8,128]{3,2,1,0:T(8,128)S(1)} %fusion.313), channel_id=1, source_target_pairs={{0,64},{8,72},{16,80},{24,88},{32,96},{40,104},{48,112},{56,120},{... | collective-permute-start | bytes 884744 | tf_op jit(solution)/shard_map/ppermute | solution.py:28
  106.6 26.5 %collective-permute-start.8 = (f32[12,6,8,128]{3,2,1,0:T(8,128)S(1)}, f32[12,6,8,128]{3,2,1,0:T(8,128)S(1)}, u32[]{:S(2)}, u32[]{:S(2)}) collective-permute-start(f32[12,6,8,128]{3,2,1,0:T(8,128)S(1)} %fusion.313), channel_id=1, source_target_pairs={{64,0},{72,8},{80,16},{88,24},{96,32},{104,40},{112,48},{120,56},{... | collective-permute-start | bytes 884744 | tf_op jit(solution)/shard_map/ppermute | solution.py:28
  107.9 9.0 collective-permute-start.10
  134.5 18.2 %collective-permute-start.15 = (f32[12,6,6,128]{3,2,1,0:T(8,128)S(1)}, f32[12,6,6,128]{3,2,1,0:T(8,128)S(1)}, u32[]{:S(2)}, u32[]{:S(2)}) collective-permute-start(f32[12,6,6,128]{3,2,1,0:T(8,128)S(1)} %get-tuple-element.23), channel_id=1, source_target_pairs={{0,8},{8,16},{16,24},{24,32},{32,40},{40,48},{48,56},{56,64},{64,7... | collective-permute-start | bytes 663560 | tf_op jit(solution)/shard_map/ppermute | solution.py:28
  136.4 27.3 %collective-permute-start.13 = (f32[12,6,8,128]{3,2,1,0:T(8,128)S(1)}, f32[12,6,8,128]{3,2,1,0:T(8,128)S(1)}, u32[]{:S(2)}, u32[]{:S(2)}) collective-permute-start(f32[12,6,8,128]{3,2,1,0:T(8,128)S(1)} %fusion.270), channel_id=1, source_target_pairs={{0,64},{8,72},{16,80},{24,88},{32,96},{40,104},{48,112},{56,120},{... | collective-permute-start | bytes 884744 | tf_op jit(solution)/shard_map/ppermute | solution.py:28
  148.6 15.2 %collective-permute-start.12 = (f32[12,6,8,128]{3,2,1,0:T(8,128)S(1)}, f32[12,6,8,128]{3,2,1,0:T(8,128)S(1)}, u32[]{:S(2)}, u32[]{:S(2)}) collective-permute-start(f32[12,6,8,128]{3,2,1,0:T(8,128)S(1)} %fusion.270), channel_id=1, source_target_pairs={{64,0},{72,8},{80,16},{88,24},{96,32},{104,40},{112,48},{120,56},{... | collective-permute-start | bytes 884744 | tf_op jit(solution)/shard_map/ppermute | solution.py:28
  149.9 13.8 %collective-permute-start.14 = (f32[12,6,6,128]{3,2,1,0:T(8,128)S(1)}, f32[12,6,6,128]{3,2,1,0:T(8,128)S(1)}, u32[]{:S(2)}, u32[]{:S(2)}) collective-permute-start(f32[12,6,6,128]{3,2,1,0:T(8,128)S(1)} %get-tuple-element.22), channel_id=1, source_target_pairs={{8,0},{16,8},{24,16},{32,24},{40,32},{48,40},{56,48},{64,56},{72,6... | collective-permute-start | bytes 663560 | tf_op jit(solution)/shard_map/ppermute | solution.py:28
  165.2 32.7 %collective-permute-start.19 = (f32[12,6,6,128]{3,2,1,0:T(8,128)S(1)}, f32[12,6,6,128]{3,2,1,0:T(8,128)S(1)}, u32[]{:S(2)}, u32[]{:S(2)}) collective-permute-start(f32[12,6,6,128]{3,2,1,0:T(8,128)S(1)} %get-tuple-element.21), channel_id=1, source_target_pairs={{0,8},{8,16},{16,24},{24,32},{32,40},{40,48},{48,56},{56,64},{64,7... | collective-permute-start | bytes 663560 | tf_op jit(solution)/shard_map/ppermute | solution.py:28
  184.3 33.3 %collective-permute-start.17 = (f32[12,6,8,128]{3,2,1,0:T(8,128)S(1)}, f32[12,6,8,128]{3,2,1,0:T(8,128)S(1)}, u32[]{:S(2)}, u32[]{:S(2)}) collective-permute-start(f32[12,6,8,128]{3,2,1,0:T(8,128)S(1)} %fusion.227), channel_id=1, source_target_pairs={{0,64},{8,72},{16,80},{24,88},{32,96},{40,104},{48,112},{56,120},{... | collective-permute-start | bytes 884744 | tf_op jit(solution)/shard_map/ppermute | solution.py:28
  194.6 33.2 %collective-permute-start.16 = (f32[12,6,8,128]{3,2,1,0:T(8,128)S(1)}, f32[12,6,8,128]{3,2,1,0:T(8,128)S(1)}, u32[]{:S(2)}, u32[]{:S(2)}) collective-permute-start(f32[12,6,8,128]{3,2,1,0:T(8,128)S(1)} %fusion.227), channel_id=1, source_target_pairs={{64,0},{72,8},{80,16},{88,24},{96,32},{104,40},{112,48},{120,56},{... | collective-permute-start | bytes 884744 | tf_op jit(solution)/shard_map/ppermute | solution.py:28
  229.2 11.1 %collective-permute-start.23 = (f32[12,6,6,128]{3,2,1,0:T(8,128)S(1)}, f32[12,6,6,128]{3,2,1,0:T(8,128)S(1)}, u32[]{:S(2)}, u32[]{:S(2)}) collective-permute-start(f32[12,6,6,128]{3,2,1,0:T(8,128)S(1)} %get-tuple-element.19), channel_id=1, source_target_pairs={{0,8},{8,16},{16,24},{24,32},{32,40},{40,48},{48,56},{56,64},{64,7... | collective-permute-start | bytes 663560 | tf_op jit(solution)/shard_map/ppermute | solution.py:28
  231.2 18.7 %collective-permute-start.21 = (f32[12,6,8,128]{3,2,1,0:T(8,128)S(1)}, f32[12,6,8,128]{3,2,1,0:T(8,128)S(1)}, u32[]{:S(2)}, u32[]{:S(2)}) collective-permute-start(f32[12,6,8,128]{3,2,1,0:T(8,128)S(1)} %fusion.184), channel_id=1, source_target_pairs={{0,64},{8,72},{16,80},{24,88},{32,96},{40,104},{48,112},{56,120},{... | collective-permute-start | bytes 884744 | tf_op jit(solution)/shard_map/ppermute | solution.py:28
  236.4 33.7 %collective-permute-start.20 = (f32[12,6,8,128]{3,2,1,0:T(8,128)S(1)}, f32[12,6,8,128]{3,2,1,0:T(8,128)S(1)}, u32[]{:S(2)}, u32[]{:S(2)}) collective-permute-start(f32[12,6,8,128]{3,2,1,0:T(8,128)S(1)} %fusion.184), channel_id=1, source_target_pairs={{64,0},{72,8},{80,16},{88,24},{96,32},{104,40},{112,48},{120,56},{... | collective-permute-start | bytes 884744 | tf_op jit(solution)/shard_map/ppermute | solution.py:28
  271.5 11.2 %collective-permute-start.27 = (f32[12,6,6,128]{3,2,1,0:T(8,128)S(1)}, f32[12,6,6,128]{3,2,1,0:T(8,128)S(1)}, u32[]{:S(2)}, u32[]{:S(2)}) collective-permute-start(f32[12,6,6,128]{3,2,1,0:T(8,128)S(1)} %get-tuple-element.17), channel_id=1, source_target_pairs={{0,8},{8,16},{16,24},{24,32},{32,40},{40,48},{48,56},{56,64},{64,7... | collective-permute-start | bytes 663560 | tf_op jit(solution)/shard_map/ppermute | solution.py:28
  273.4 15.3 %collective-permute-start.25 = (f32[12,6,8,128]{3,2,1,0:T(8,128)S(1)}, f32[12,6,8,128]{3,2,1,0:T(8,128)S(1)}, u32[]{:S(2)}, u32[]{:S(2)}) collective-permute-start(f32[12,6,8,128]{3,2,1,0:T(8,128)S(1)} %fusion.141), channel_id=1, source_target_pairs={{0,64},{8,72},{16,80},{24,88},{32,96},{40,104},{48,112},{56,120},{... | collective-permute-start | bytes 884744 | tf_op jit(solution)/shard_map/ppermute | solution.py:28
  278.7 33.5 %collective-permute-start.24 = (f32[12,6,8,128]{3,2,1,0:T(8,128)S(1)}, f32[12,6,8,128]{3,2,1,0:T(8,128)S(1)}, u32[]{:S(2)}, u32[]{:S(2)}) collective-permute-start(f32[12,6,8,128]{3,2,1,0:T(8,128)S(1)} %fusion.141), channel_id=1, source_target_pairs={{64,0},{72,8},{80,16},{88,24},{96,32},{104,40},{112,48},{120,56},{... | collective-permute-start | bytes 884744 | tf_op jit(solution)/shard_map/ppermute | solution.py:28
  313.5 11.7 %collective-permute-start.31 = (f32[12,6,6,128]{3,2,1,0:T(8,128)S(1)}, f32[12,6,6,128]{3,2,1,0:T(8,128)S(1)}, u32[]{:S(2)}, u32[]{:S(2)}) collective-permute-start(f32[12,6,6,128]{3,2,1,0:T(8,128)S(1)} %get-tuple-element.15), channel_id=1, source_target_pairs={{0,8},{8,16},{16,24},{24,32},{32,40},{40,48},{48,56},{56,64},{64,7... | collective-permute-start | bytes 663560 | tf_op jit(solution)/shard_map/ppermute | solution.py:28
  315.5 19.7 %collective-permute-start.29 = (f32[12,6,8,128]{3,2,1,0:T(8,128)S(1)}, f32[12,6,8,128]{3,2,1,0:T(8,128)S(1)}, u32[]{:S(2)}, u32[]{:S(2)}) collective-permute-start(f32[12,6,8,128]{3,2,1,0:T(8,128)S(1)} %fusion.98), channel_id=1, source_target_pairs={{0,64},{8,72},{16,80},{24,88},{32,96},{40,104},{48,112},{56,120},{... | collective-permute-start | bytes 884744 | tf_op jit(solution)/shard_map/ppermute | solution.py:28
  321.2 32.5 %collective-permute-start.28 = (f32[12,6,8,128]{3,2,1,0:T(8,128)S(1)}, f32[12,6,8,128]{3,2,1,0:T(8,128)S(1)}, u32[]{:S(2)}, u32[]{:S(2)}) collective-permute-start(f32[12,6,8,128]{3,2,1,0:T(8,128)S(1)} %fusion.98), channel_id=1, source_target_pairs={{64,0},{72,8},{80,16},{88,24},{96,32},{104,40},{112,48},{120,56},{... | collective-permute-start | bytes 884744 | tf_op jit(solution)/shard_map/ppermute | solution.py:28
  322.5 12.7 %collective-permute-start.30 = (f32[12,6,6,128]{3,2,1,0:T(8,128)S(1)}, f32[12,6,6,128]{3,2,1,0:T(8,128)S(1)}, u32[]{:S(2)}, u32[]{:S(2)}) collective-permute-start(f32[12,6,6,128]{3,2,1,0:T(8,128)S(1)} %get-tuple-element.14), channel_id=1, source_target_pairs={{8,0},{16,8},{24,16},{32,24},{40,32},{48,40},{56,48},{64,56},{72,6... | collective-permute-start | bytes 663560 | tf_op jit(solution)/shard_map/ppermute | solution.py:28
  355.9 525.7 %all-reduce.12.cloned.1.call-start = ((), (), s32[]{:S(2)}) async-start(), calls=%async_computation.1 | async-start | bytes 196608 | tf_op jit(solution)/shard_map/psum | solution.py:94
  356.0 14.7 %collective-permute-start.35 = (f32[12,6,6,128]{3,2,1,0:T(8,128)S(1)}, f32[12,6,6,128]{3,2,1,0:T(8,128)S(1)}, u32[]{:S(2)}, u32[]{:S(2)}) collective-permute-start(f32[12,6,6,128]{3,2,1,0:T(8,128)S(1)} %get-tuple-element.13), channel_id=1, source_target_pairs={{0,8},{8,16},{16,24},{24,32},{32,40},{40,48},{48,56},{56,64},{64,7... | collective-permute-start | bytes 663560 | tf_op jit(solution)/shard_map/ppermute | solution.py:28
  357.9 21.2 %collective-permute-start.33 = (f32[12,6,8,128]{3,2,1,0:T(8,128)S(1)}, f32[12,6,8,128]{3,2,1,0:T(8,128)S(1)}, u32[]{:S(2)}, u32[]{:S(2)}) collective-permute-start(f32[12,6,8,128]{3,2,1,0:T(8,128)S(1)} %fusion.55), channel_id=1, source_target_pairs={{0,64},{8,72},{16,80},{24,88},{32,96},{40,104},{48,112},{56,120},{... | collective-permute-start | bytes 884744 | tf_op jit(solution)/shard_map/ppermute | solution.py:28
  366.4 33.3 %collective-permute-start.32 = (f32[12,6,8,128]{3,2,1,0:T(8,128)S(1)}, f32[12,6,8,128]{3,2,1,0:T(8,128)S(1)}, u32[]{:S(2)}, u32[]{:S(2)}) collective-permute-start(f32[12,6,8,128]{3,2,1,0:T(8,128)S(1)} %fusion.55), channel_id=1, source_target_pairs={{64,0},{72,8},{80,16},{88,24},{96,32},{104,40},{112,48},{120,56},{... | collective-permute-start | bytes 884744 | tf_op jit(solution)/shard_map/ppermute | solution.py:28
  (11 other events, 157.0 us)
Sparse Core Ops, SparseCore 0:
  356.0 76.5 all-gather.2
  440.1 441.4 all-reduce.11
where the time goes:
time: 912 us; the launch traced here: 911 us
  waiting for transfers between devices  705 us (77%)
  starting transfers between devices  147 us (16%)
  other arithmetic  31.4 us (3%)
  between operations  14.9 us (2%)
    psum x1, waiting for transfers between devices, local(): over_sum, proj_sum = lax.psum((over_part, proj_part), ('dom', 'orb'))  442 us
    ppermute x36, waiting for transfers between devices, from_behind(): lax.ppermute(value, axis, [(source, source + steps) for source in range(i...  231 us
    ppermute x36, starting transfers between devices, from_behind(): lax.ppermute(value, axis, [(source, source + steps) for source in range(i...  147 us
    all_gather x1, waiting for transfers between devices, local(): piece = lax.all_gather(flat_f, 'orb', axis=0, tiled=True)  31.5 us
  transfers between devices with their start and end apart: 38, of which 24 were waited for; matrix products, arithmetic and copies ran while one was open for 0% of the time, Pallas kernels for 0%

commit v1 on v0

v1 whole, which is shorter than its diff:
```python
import jax
import jax.numpy as jnp
import numpy as np
from jax import lax
from jax.experimental import pallas as pl
from jax.experimental.pallas import tpu as pltpu
from jax.sharding import PartitionSpec as P

MESH = pl.DeviceIdType.MESH
HI = lax.Precision.HIGHEST

NORB = 96
DEGREE = 8
RADIUS = 6
CELLS = 48 * 64 * 128

COEF = (
    -5369.0 / 1800.0,
    12.0 / 7.0,
    -15.0 / 56.0,
    10.0 / 189.0,
    -1.0 / 112.0,
    2.0 / 1925.0,
    -1.0 / 16632.0,
)
E_HALF = 6.0
CENTER = 8.0
A_LOW = 0.0

ROWS = 24
EXT_ROWS = ROWS + 2 * RADIUS
EXT_COLS = 80


def z_weights():
    w = np.zeros((128, 128), np.float64)
    for k in range(-RADIUS, RADIUS + 1):
        w += np.diag(np.full(128 - abs(k), COEF[abs(k)]), k)
    w += 2.0 * COEF[0] * np.eye(128)
    return (-0.5 * w).astype(np.float32)


def step_scalars():
    rows = [(0.0, 0.0, 0.0)]
    sigma = sigma_one = E_HALF / (A_LOW - CENTER)
    rows.append((sigma_one / E_HALF, CENTER, 0.0))
    for _ in range(2, DEGREE + 1):
        sigma_next = 1.0 / (2.0 / sigma_one - sigma)
        rows.append((2.0 * sigma_next / E_HALF, CENTER, sigma * sigma_next))
        sigma = sigma_next
    rows.append((1.0, 0.0, 0.0))
    return np.asarray(rows, np.float32).reshape(-1)


def place():
    d, o = lax.axis_index("dom"), lax.axis_index("orb")
    y_lo, z, c = d // 32, (d // 2) % 16, d % 2
    off = jnp.maximum(z - y_lo, 0)
    slot = (off * 3 + 2) // 8
    active = (z >= y_lo) & (slot < 6) & ((slot * 8) // 3 == off)
    return d, o, y_lo, z, c, slot, active


def holder(j, c):
    y_lo, slot = j % 2, j // 2
    return y_lo * 32 + ((slot * 8) // 3 + y_lo) * 2 + c


def copy_to(src, dst, send, recv, **axes):
    return pltpu.make_async_remote_copy(
        src_ref=src, dst_ref=dst, send_sem=send, recv_sem=recv, device_id=axes, device_id_type=MESH
    )


def landed(ref, sem):
    pltpu.make_async_copy(ref, ref, sem).wait()


def loop(n, body):
    lax.fori_loop(0, n, lambda i, carry: (body(i), carry)[1], 0)


def filter_kernel(
    scal_ref, orb_ref, pot_ref, w_ref, fall_ref, gram_ref,
    buf, potb, zs, fback, aback, fall, aall,
    in_send, in_recv, p_send, p_recv, g_send, g_recv, h_send, h_recv,
    f_send, f_recv, a_send, a_recv, rf_send, rf_recv, ra_send, ra_recv,
):
    d, o, y_lo, z, c, slot, active = place()
    orbital = slot * 2 + y_lo
    prow, pcol = d // 8, d % 8
    selfpair = active & (c == y_lo)

    @pl.when(active)
    def _():
        zero = jnp.zeros((EXT_COLS, 128), jnp.float32)

        def clear(i):
            buf[0, i] = zero
            buf[1, i] = zero

        loop(EXT_ROWS, clear)

    barrier = pltpu.get_barrier_semaphore()

    def greet(cond, **axes):
        @pl.when(cond)
        def _():
            pl.semaphore_signal(barrier, inc=1, device_id=axes, device_id_type=MESH)

    def greet_holder(j):
        t = holder(j, y_lo)
        greet(t != d, dom=t)

    def greet_orb(b):
        greet(b != o, orb=b)

    def greet_source(m):
        t = c * 32 + m
        greet(t != d, dom=t)

    loop(12, greet_holder)
    loop(8, greet_orb)

    @pl.when(active)
    def _():
        loop(32, greet_source)
        pl.semaphore_signal(barrier, inc=1, device_id={"dom": d + 1 - 2 * c}, device_id_type=MESH)

    pl.semaphore_wait(barrier, 19 + 33 * active.astype(jnp.int32) - 2 * selfpair.astype(jnp.int32))

    col0 = pl.multiple_of(pcol * 8, 8)

    def pot_copy(j):
        return copy_to(
            pot_ref.at[0, o], potb.at[prow % 4, o, pl.ds(col0, 8)], p_send.at[j], p_recv, dom=holder(j, y_lo)
        )

    def send_pot(i):
        j = (i + z) % 12

        @pl.when(holder(j, y_lo) != d)
        def _():
            pot_copy(j).start()

        @pl.when(holder(j, y_lo) == d)
        def _():
            pltpu.make_async_copy(pot_ref.at[0, o], potb.at[prow % 4, o, pl.ds(col0, 8)], p_recv).start()

    @pl.when(o < 6)
    def _():
        loop(12, send_pot)

    def in_dst():
        return buf.at[0, pl.ds(RADIUS + (prow % 4) * 6, 6), pl.ds(pl.multiple_of(8 + pcol * 8, 8), 8)]

    def in_copy(j):
        return copy_to(orb_ref.at[j, 0], in_dst(), in_send.at[j], in_recv, dom=holder(j, y_lo))

    def send_in(i):
        j = (i + z) % 12

        @pl.when(holder(j, y_lo) != d)
        def _():
            in_copy(j).start()

        @pl.when(holder(j, y_lo) == d)
        def _():
            pltpu.make_async_copy(orb_ref.at[j, 0], in_dst(), in_recv).start()

    loop(12, send_in)

    def share_copy(b):
        return copy_to(potb.at[:, o], potb.at[:, o], g_send.at[b], g_recv.at[o], orb=b)

    def out_src(m, at):
        q, col = m // 8, m % 8
        return buf.at[at, pl.ds(RADIUS + q * 6, 6), pl.ds(pl.multiple_of(8 + col * 8, 8), 8)]

    def send_out(at, back, send, recv):
        def one(i):
            m = (i + d) % 32
            t = c * 32 + m

            @pl.when(t != d)
            def _():
                copy_to(out_src(m, at), back.at[orbital], send.at[m], recv, dom=t).start()

            @pl.when(t == d)
            def _():
                pltpu.make_async_copy(out_src(m, at), back.at[orbital], recv).start()

        loop(32, one)

    def sent_out(at, back, send, recv):
        def one(m):
            t = c * 32 + m

            @pl.when(t != d)
            def _():
                copy_to(out_src(m, at), back.at[orbital], send.at[m], recv, dom=t).wait_send()

        loop(32, one)

    @pl.when(active)
    def _():
        @pl.when(o < 6)
        def _():
            landed(potb.at[:, 0], p_recv)

            def share(b):
                @pl.when(b != o)
                def _():
                    share_copy(b).start()

            loop(8, share)

        def shared(r):
            @pl.when(r != o)
            def _():
                landed(potb.at[:, 0], g_recv.at[r])

        loop(6, shared)
        landed(buf.at[0, pl.ds(RADIUS, ROWS), pl.ds(8, 64)], in_recv)

        def step(s):
            cur, new = (s + 1) % 2, s % 2
            halo = copy_to(
                buf.at[cur, pl.ds(24 - 18 * c, 6), pl.ds(8, 64)],
                buf.at[cur, pl.ds(30 * c, 6), pl.ds(8, 64)],
                h_send.at[cur], h_recv.at[cur], dom=d + 1 - 2 * c,
            )
            halo.start()
            scale, shift, past = scal_ref[3 * s], scal_ref[3 * s + 1], scal_ref[3 * s + 2]

            def block(i):
                @pl.when(i == 3)
                def _():
                    halo.wait_recv()

                blk = jnp.where(c == 0, i, 3 - i)
                r0 = RADIUS + blk * 6
                x = buf[cur, pl.ds(r0, 6), 8:72, :].reshape(6 * 64, 128)
                zs[...] = jnp.dot(
                    x, w_ref[...], precision=HI, preferred_element_type=jnp.float32
                ).reshape(6, 64, 128)
                for yt in range(8):
                    y0 = 8 + 8 * yt
                    col = [buf[cur, r0 - RADIUS + m, y0 : y0 + 8, :] for m in range(18)]
                    for i6 in range(6):
                        r = r0 + i6
                        acc = zs[i6, y0 - 8 : y0, :]
                        mid = col[i6 + RADIUS]
                        for k in range(1, RADIUS + 1):
                            term = col[i6 + RADIUS + k] + col[i6 + RADIUS - k]
                            term = term + (
                                buf[cur, r, y0 + k : y0 + k + 8, :] + buf[cur, r, y0 - k : y0 - k + 8, :]
                            )
                            acc = acc + (-0.5 * COEF[k]) * term
                        acc = acc + (potb[blk, i6, y0 - 8 : y0, :] - shift) * mid
                        buf[new, r, y0 : y0 + 8, :] = scale * acc - past * buf[new, r, y0 : y0 + 8, :]

            loop(4, block)
            halo.wait_send()

            @pl.when(s == DEGREE)
            def _():
                send_out(0, fback, f_send, f_recv)

        loop(DEGREE + 1, lambda s: step(s + 1))
        send_out(1, aback, a_send, a_recv)

    def meet_copy(back, every, send, recv, r):
        return copy_to(back.at[:, r], every.at[pl.ds(o * 12, 12)], send.at[r], recv, orb=(r + z) % 8)

    def send_meet(back, every, send, recv):
        def one(r):
            @pl.when((r + z) % 8 != o)
            def _():
                meet_copy(back, every, send, recv, r).start()

            @pl.when((r + z) % 8 == o)
            def _():
                pltpu.make_async_copy(back.at[:, r], every.at[pl.ds(o * 12, 12)], recv).start()

        loop(6, one)

    def sent_meet(back, every, send, recv):
        def one(r):
            @pl.when((r + z) % 8 != o)
            def _():
                meet_copy(back, every, send, recv, r).wait_send()

        loop(6, one)

    landed(fback, f_recv)
    send_meet(fback, fall, rf_send, rf_recv)
    landed(aback, a_recv)
    send_meet(aback, aall, ra_send, ra_recv)

    meets = (o + 16 - z) % 8 < 6

    @pl.when(meets)
    def _():
        landed(fall, rf_recv)
        landed(aall, ra_recv)
        over = jnp.zeros((NORB, NORB), jnp.float32)
        proj = jnp.zeros((NORB, NORB), jnp.float32)
        dims = (((1,), (1,)), ((), ()))
        for s in range(8):
            f, a = fall[:, s, :], aall[:, s, :]
            over = over + lax.dot_general(f, f, dims, precision=HI, preferred_element_type=jnp.float32)
            proj = proj + lax.dot_general(f, a, dims, precision=HI, preferred_element_type=jnp.float32)
        gram_ref[...] = jnp.zeros_like(gram_ref)
        gram_ref[0:NORB, 0:NORB] = over
        gram_ref[NORB : 2 * NORB, 0:NORB] = proj
        fall_ref[...] = fall[...]

    @pl.when(jnp.logical_not(meets))
    def _():
        gram_ref[...] = jnp.zeros_like(gram_ref)
        fall_ref[...] = jnp.zeros_like(fall_ref)

    sent_meet(fback, fall, rf_send, rf_recv)
    sent_meet(aback, aall, ra_send, ra_recv)

    def sent_in(j):
        @pl.when(holder(j, y_lo) != d)
        def _():
            in_copy(j).wait_send()

            @pl.when(o < 6)
            def _():
                pot_copy(j).wait_send()

    loop(12, sent_in)

    @pl.when(active)
    def _():
        @pl.when(o < 6)
        def _():
            def one(b):
                @pl.when(b != o)
                def _():
                    share_copy(b).wait_send()

            loop(8, one)

        sent_out(0, fback, f_send, f_recv)
        sent_out(1, aback, a_send, a_recv)


def greet_groups(groups):
    barrier = pltpu.get_barrier_semaphore()
    for size, me, axes in groups:
        def one(b, me=me, axes=axes):
            @pl.when(b != me)
            def _():
                pl.semaphore_signal(barrier, inc=1, device_id=axes(b), device_id_type=MESH)

        loop(size, one)
    pl.semaphore_wait(barrier, sum(size - 1 for size, _, _ in groups))


def sum_kernel(g_ref, out_ref, part, ra, rb, rc, full, *sems):
    d, o = lax.axis_index("dom"), lax.axis_index("orb")
    low, high = d % 8, d // 8
    in_orb = (8, o, lambda b: {"orb": b})
    in_low = (8, low, lambda b: {"dom": high * 8 + b})
    in_high = (8, high, lambda b: {"dom": b * 8 + low})
    greet_groups((in_orb, in_low, in_high))
    waits = []

    def exchange(group, src, slots, send, recv):
        size, me, axes = group

        def each(do):
            def one(b):
                @pl.when(b != me)
                def _():
                    do(copy_to(src(b), slots.at[me], send.at[b], recv, **axes(b)))

            loop(size, one)

        each(lambda copy: copy.start())
        waits.append(lambda: each(lambda copy: copy.wait_send()))
        landed(slots.at[pl.ds(0, size - 1)], recv)

    def total(slots):
        acc = slots[0]
        for b in range(1, 8):
            acc = acc + slots[b]
        return acc

    mine = pl.multiple_of(o * 24, 8)
    ra[o] = g_ref[pl.ds(mine, 24), :]
    exchange(in_orb, lambda b: g_ref.at[pl.ds(pl.multiple_of(b * 24, 8), 24)], ra, sems[0], sems[1])
    part[0] = total(ra)
    rb[low] = part[0]
    exchange(in_low, lambda b: part.at[0], rb, sems[2], sems[3])
    part[1] = total(rb)
    rc[high] = part[1]
    exchange(in_high, lambda b: part.at[1], rc, sems[4], sems[5])
    part[2] = total(rc)
    full[o] = part[2]
    exchange(in_orb, lambda b: part.at[2], full, sems[6], sems[7])
    out_ref[...] = full[...].reshape(192, 128)
    for wait in waits:
        wait()


def rotate_kernel(inv_ref, fall_ref, out_ref, rot, send, recv):
    d, o = lax.axis_index("dom"), lax.axis_index("orb")
    z = (d // 2) % 16
    greet_groups(((8, o, lambda b: {"orb": b}),))
    r = (o + 16 - z) % 8

    def copy(b):
        return copy_to(rot.at[pl.ds(b * 12, 12)], out_ref.at[:, 0, r], send.at[b], recv, orb=b)

    @pl.when(r < 6)
    def _():
        inv = inv_ref[...]
        for s in range(8):
            rot[:, s, :] = jnp.dot(inv, fall_ref[:, s, :], precision=HI, preferred_element_type=jnp.float32)

        def one(b):
            @pl.when(b != o)
            def _():
                copy(b).start()

            @pl.when(b == o)
            def _():
                pltpu.make_async_copy(rot.at[pl.ds(b * 12, 12)], out_ref.at[:, 0, r], recv).start()

        loop(8, one)

    landed(out_ref, recv)

    @pl.when(r < 6)
    def _():
        def one(b):
            @pl.when(b != o)
            def _():
                copy(b).wait_send()

        loop(8, one)


def local(orbitals, potential):
    f32 = jnp.float32
    vmem, anyspace = pl.BlockSpec(memory_space=pltpu.VMEM), pl.BlockSpec(memory_space=pl.ANY)
    dma = pltpu.SemaphoreType.DMA
    fall, gram = pl.pallas_call(
        filter_kernel,
        out_shape=(
            jax.ShapeDtypeStruct((NORB, 8, 128), f32),
            jax.ShapeDtypeStruct((2 * NORB, 128), f32),
        ),
        in_specs=[pl.BlockSpec(memory_space=pltpu.SMEM), anyspace, anyspace, vmem],
        out_specs=(vmem, vmem),
        scratch_shapes=[
            pltpu.VMEM((2, EXT_ROWS, EXT_COLS, 128), f32),
            pltpu.VMEM((4, 6, 64, 128), f32),
            pltpu.VMEM((6, 64, 128), f32),
            pltpu.VMEM((12, 6, 8, 128), f32),
            pltpu.VMEM((12, 6, 8, 128), f32),
            pltpu.VMEM((NORB, 8, 128), f32),
            pltpu.VMEM((NORB, 8, 128), f32),
            dma((12,)), dma, dma((12,)), dma, dma((8,)), dma((6,)), dma((2,)), dma((2,)),
            dma((32,)), dma, dma((32,)), dma, dma((6,)), dma, dma((6,)), dma,
        ],
        compiler_params=pltpu.CompilerParams(
            collective_id=0, has_side_effects=True, vmem_limit_bytes=32 * 2**20
        ),
        name="filter_orbitals",
    )(jnp.asarray(step_scalars()), orbitals, potential, jnp.asarray(z_weights()))
    total = pl.pallas_call(
        sum_kernel,
        out_shape=jax.ShapeDtypeStruct((2 * NORB, 128), f32),
        in_specs=[vmem],
        out_specs=vmem,
        scratch_shapes=[pltpu.VMEM((3, 24, 128), f32)]
        + [pltpu.VMEM((8, 24, 128), f32)] * 4
        + [dma((8,)), dma] * 4,
        compiler_params=pltpu.CompilerParams(collective_id=1, has_side_effects=True),
        name="sum_over_devices",
    )(gram)
    intersection = total[:NORB, :NORB] / float(CELLS)
    projected = total[NORB:, :NORB] / float(CELLS)
    lower = jnp.linalg.cholesky(intersection)
    inverse = lax.linalg.triangular_solve(lower, jnp.eye(NORB, dtype=f32), left_side=True, lower=True)
    subspace_h = jnp.dot(jnp.dot(inverse, projected, precision=HI), inverse.T, precision=HI)
    rotated = pl.pallas_call(
        rotate_kernel,
        out_shape=jax.ShapeDtypeStruct(orbitals.shape, f32),
        in_specs=[vmem, vmem],
        out_specs=anyspace,
        scratch_shapes=[pltpu.VMEM((NORB, 8, 128), f32), dma((8,)), dma],
        compiler_params=pltpu.CompilerParams(collective_id=2, has_side_effects=True),
        name="rotate_orbitals",
    )(inverse, fall)
    return (rotated, subspace_h)


def solution(mesh):
    return jax.shard_map(
        local,
        mesh=mesh,
        in_specs=(P("orb", "dom", None, None, None), P("dom", None, None, None)),
        out_specs=(P("orb", "dom", None, None, None), P()),
        check_vma=False,
    )
```

time: 912 us -> 197 us (0.22)
  the two profiles are of different devices: /device:TPU:1 before, /device:TPU:24 now
where the time goes in v1:
time: 197 us; the launch traced here: 196 us
  Pallas kernels  170 us (86%)
  other arithmetic  17.5 us (9%)
  local copies, waits for them, and re-layouts  6.36 us (3%)
    pallas_call x1, Pallas kernels, local(): pl.pallas_call(filter_kernel, out_shape=(jax.ShapeDtypeStruct((NORB, 8, 1...  122 us
    pallas_call x1, Pallas kernels, local(): pl.pallas_call(sum_kernel, out_shape=jax.ShapeDtypeStruct((2 * NORB, 128)...  36 us
    pallas_call x1, Pallas kernels, local(): pl.pallas_call(rotate_kernel, out_shape=jax.ShapeDtypeStruct(orbitals.sha...  12 us
    another operation x3, other arithmetic, local(): lower = jnp.linalg.cholesky(intersection)  9.45 us
    another operation x2, other arithmetic, local(): lax.linalg.triangular_solve(lower, jnp.eye(NORB, dtype=f32), left_side=Tr...  8.01 us
    unnamed x19, local copies, waits for them, and re-layouts  5.45 us

profile of v1, /device:TPU:24, one launch (start us, length us, event | category | flops | bytes accessed | tf_op | source)
XLA Modules:
  0.0 196.2 jit_solution(2519831044568361804)
XLA Ops:
  0.6 0.0 copy-start.1
  0.6 1.0 copy-done.1
  1.6 0.0 copy-start.3
  1.6 0.8 copy-done.3
  2.4 0.0 copy-start.4
  2.4 0.7 copy-done.4
  3.2 0.0 copy-start.5
  3.2 0.7 copy-done.5
  3.8 121.7 %filter_orbitals.1 = (f32[96,8,128]{2,1,0:T(8,128)S(1)}, f32[192,128]{1,0:T(8,128)S(1)}) custom-call(f32[30]{0:T(128)S(1)} %copy-done.5, f32[12,1,6,8,128]{4,3,2,1,0:T(8,128)S(1)} %copy-done.1, f32[1,6,8,128]{3,2,1,0:T(8,128)S(1)} %copy-done.4, f32[128,128]{1,0:T(8,128)S(1)} %copy-done.3), custom_call_target="tpu_custom_call" | custom-call | tf_op jit(solution)/shard_map/filter_orbitals/pallas_call | solution.py:454
  125.5 0.0 copy-start
  125.5 0.7 copy-done
  126.3 0.0 copy-start.2
  126.3 0.6 copy-done.2
  126.9 36.0 %sum_over_devices.1 = f32[192,128]{1,0:T(8,128)} custom-call(f32[192,128]{1,0:T(8,128)} %copy-done.2), custom_call_target="tpu_custom_call" | custom-call | tf_op jit(solution)/shard_map/sum_over_devices/pallas_call | solution.py:478
  162.9 0.8 fusion.8
  163.7 0.1 copy.10
  163.8 0.1 copy.9
  163.9 0.1 copy.7
  164.0 8.8 %cholesky.17 = f32[96,96]{1,0:T(8,128)S(1)} custom-call(f32[96,96]{1,0:T(8,128)S(1)} %fusion.3), custom_call_target="Cholesky" | custom-call | tf_op jit(solution)/shard_map/jit(cholesky)/cholesky | solution.py:491
  172.8 0.6 compare_reduce_fusion
  173.4 0.7 fusion
  174.1 7.4 %custom-call.6 = f32[1,96,96]{1,2,0:T(8,128)S(1)} custom-call(f32[1,96,96]{2,1,0:T(8,128)S(1)} %fusion), custom_call_target="InvertDiagBlocksLowerTriangular" | custom-call | tf_op jit(solution)/shard_map/triangular_solve | solution.py:492
  181.5 0.9 fusion.1.inv_ref
  182.3 0.0 copy-start.7
  182.3 12.0 %rotate_orbitals.1 = f32[12,1,6,8,128]{4,3,2,1,0:T(8,128)} custom-call(f32[96,96]{1,0:T(8,128)} %fusion.1.inv_ref, f32[96,8,128]{2,1,0:T(8,128)} %copy-done), custom_call_target="tpu_custom_call" | custom-call | tf_op jit(solution)/shard_map/rotate_orbitals/pallas_call | solution.py:494
  194.3 0.0 copy-done.7
  194.4 0.0 copy-start.6
  194.4 0.2 fusion.4
  194.6 0.8 fusion.9
  195.4 0.0 copy-done.6
  195.4 0.7 copy.12
  (3 shorter events, 0.1 us)
Async XLA Ops:
  0.6 1.0 copy-start.1
  1.6 0.8 copy-start.3
  2.4 0.7 copy-start.4
  3.2 0.7 copy-start.5
  125.5 0.7 copy-start
  126.3 0.6 copy-start.2
  182.3 12.0 %copy-start.7 = (f32[96,96]{1,0:T(8,128)S(1)}, f32[96,96]{1,0:T(8,128)}, u32[]{:S(2)}) copy-start(f32[96,96]{1,0:T(8,128)} %fusion.1.inv_ref) | copy-start | bytes 110596
  194.4 1.1 copy-start.6

commit v2 on v0

v2 whole, which is shorter than its diff:
```python
import jax
import jax.numpy as jnp
from jax import lax
from jax.experimental import pallas as pl
from jax.experimental.pallas import tpu as pltpu
from jax.sharding import PartitionSpec as P

MESH = pl.DeviceIdType.MESH
HI = lax.Precision.HIGHEST
F32 = jnp.float32

NORB = 96
DEGREE = 8
RADIUS = 6
CELLS = 48 * 64 * 128

COEF = (
    -5369.0 / 1800.0,
    12.0 / 7.0,
    -15.0 / 56.0,
    10.0 / 189.0,
    -1.0 / 112.0,
    2.0 / 1925.0,
    -1.0 / 16632.0,
)
E_HALF = 6.0
CENTER = 8.0
A_LOW = 0.0

ROWS = 24
EXT_ROWS = ROWS + 2 * RADIUS
EXT_COLS = 80


def step_scalars():
    rows = [(0.0, 0.0, 0.0)]
    sigma = sigma_one = E_HALF / (A_LOW - CENTER)
    rows.append((sigma_one / E_HALF, CENTER, 0.0))
    for _ in range(2, DEGREE + 1):
        sigma_next = 1.0 / (2.0 / sigma_one - sigma)
        rows.append((2.0 * sigma_next / E_HALF, CENTER, sigma * sigma_next))
        sigma = sigma_next
    rows.append((1.0, 0.0, 0.0))
    return rows


def holder(j, c):
    y_lo, slot = j % 2, j // 2
    return y_lo * 32 + ((slot * 8) // 3 + y_lo) * 2 + c


def copy_to(src, dst, send, recv, axes):
    return pltpu.make_async_remote_copy(
        src_ref=src, dst_ref=dst, send_sem=send, recv_sem=recv, device_id=axes, device_id_type=MESH
    )


def landed(ref, sem):
    pltpu.make_async_copy(ref, ref, sem).wait()


def loop(n, body):
    lax.fori_loop(0, n, lambda i, carry: (body(i), carry)[1], 0)


def when(cond):
    return pl.when(cond)


def over_lanes(tile, j):
    return jnp.broadcast_to(tile[:, j : j + 1], (8, 128))


def over_rows(tile, r):
    return jnp.broadcast_to(tile[r : r + 1, :], (8, 128))


def inverse_factor(matrix):
    sub = lax.broadcasted_iota(jnp.int32, (8, 128), 0)
    lane = lax.broadcasted_iota(jnp.int32, (8, 128), 1)
    tiles = NORB // 8
    st = [matrix[8 * t : 8 * t + 8, :] for t in range(tiles)]
    et = [jnp.where(lane == sub + 8 * t, 1.0, 0.0).astype(F32) for t in range(tiles)]
    for j in range(0, NORB, 2):
        t0, r = divmod(j, 8)
        c0 = [over_lanes(st[t], j) for t in range(t0, tiles)]
        c1 = [over_lanes(st[t], j + 1) for t in range(t0, tiles)]
        a, b, c = over_rows(c0[0], r), over_rows(c0[0], r + 1), over_rows(c1[0], r + 1)
        s0, s1 = over_rows(st[t0], r), over_rows(st[t0], r + 1)
        e0, e1 = over_rows(et[t0], r), over_rows(et[t0], r + 1)
        inv_a = 1.0 / a
        q = b * inv_a
        d = c - b * q
        inv_d = 1.0 / d
        s1 = (s1 - q * s0) * inv_d
        e1 = e1 - q * e0
        s0 = s0 * inv_a
        e0d, e1d = e0 * inv_a, e1 * inv_d
        for t in range(t0, tiles):
            m0 = c0[t - t0]
            m1 = c1[t - t0] - m0 * q
            if t == t0:
                m0, m1 = jnp.where(sub > r + 1, m0, 0.0), jnp.where(sub > r + 1, m1, 0.0)
            st[t] = st[t] - m0 * s0 - m1 * s1
            et[t] = et[t] - m0 * e0d - m1 * e1d
        et[t0] = jnp.where(
            sub == r, e0 * lax.rsqrt(a), jnp.where(sub == r + 1, e1 * lax.rsqrt(d), et[t0])
        )
    return jnp.concatenate(et, axis=0)


def kernel(
    orb_ref, pot_ref, out_ref, sub_ref,
    buf, potb, zs, w, scal, back, every, gram, r1, r2, mine, full, rot,
    in_send, in_recv, p_send, p_recv, g_send, g_recv, h_send, h_recv, b_send, b_recv, m_send, m_recv,
    r1_send, r1_recv, r2_send, r2_recv, r3_send, full_recv, o_send, o_recv,
):
    d, o = lax.axis_index("dom"), lax.axis_index("orb")
    y_lo, z, c = d // 32, (d // 2) % 16, d % 2
    prow, pcol = d // 8, d % 8
    off = jnp.maximum(z - y_lo, 0)
    slot = (off * 3 + 2) // 8
    active = (z >= y_lo) & (slot < 6) & ((slot * 8) // 3 == off)
    orbital = slot * 2 + y_lo
    selfpair = active & (c == y_lo)
    meet_row = (o + 16 - z) % 8
    meets = meet_row < 6
    tile = y_lo * 8 + o
    owns = tile < 12

    barrier = pltpu.get_barrier_semaphore()

    def greet(cond, axes):
        @when(cond)
        def _():
            pl.semaphore_signal(barrier, inc=1, device_id=axes, device_id_type=MESH)

    def start(here, src, dst, send, recv, axes):
        @when(here)
        def _():
            pltpu.make_async_copy(src, dst, recv).start()

        @when(jnp.logical_not(here))
        def _():
            copy_to(src, dst, send, recv, axes).start()

    def left(here, src, dst, send, recv, axes):
        @when(jnp.logical_not(here))
        def _():
            copy_to(src, dst, send, recv, axes).wait_send()

    @when(active)
    def _():
        loop(32, lambda m: greet(c * 32 + m != d, {"dom": c * 32 + m}))

    loop(12, lambda j: greet(holder(j, y_lo) != d, {"dom": holder(j, y_lo)}))
    loop(8, lambda b: greet(b != o, {"orb": b}))

    partner = {"dom": d + 1 - 2 * c}

    @when(active)
    def _():
        margin, side = jnp.zeros((EXT_COLS, 128), F32), jnp.zeros((8, 128), F32)

        def clear(i):
            buf[1, i] = margin
            buf[0, i, 0:8, :] = side
            buf[0, i, 72:80, :] = side

        loop(EXT_ROWS, clear)

        def clear_rows(i):
            buf[0, i] = margin
            buf[0, i + EXT_ROWS - RADIUS] = margin

        loop(RADIUS, clear_rows)
        gap = jnp.abs(
            lax.broadcasted_iota(jnp.int32, (128, 128), 0) - lax.broadcasted_iota(jnp.int32, (128, 128), 1)
        )
        weights = jnp.where(gap == 0, -1.5 * COEF[0], 0.0)
        for k in range(1, RADIUS + 1):
            weights = jnp.where(gap == k, -0.5 * COEF[k], weights)
        w[...] = weights.astype(F32)
        for s, row in enumerate(step_scalars()):
            for i, value in enumerate(row):
                scal[3 * s + i] = jnp.float32(value)
        greet(active, partner)

    pl.semaphore_wait(barrier, 19 + 33 * active.astype(jnp.int32) - 2 * selfpair.astype(jnp.int32))

    far = (((z + 8) % 16) * 3) // 4
    col0 = pl.multiple_of(pcol * 8, 8)

    def far_first(i):
        return (far + 12 + jnp.where(i % 2 == 0, -(i // 2), (i + 1) // 2)) % 12

    def pot_args(j):
        t = holder(j, y_lo)
        return t == d, pot_ref.at[0, o], potb.at[prow % 4, o, pl.ds(col0, 8)], p_send.at[j], p_recv.at[prow % 4], {"dom": t}

    def in_args(j):
        t = holder(j, y_lo)
        dst = buf.at[0, pl.ds(RADIUS + (prow % 4) * 6, 6), pl.ds(pl.multiple_of(8 + pcol * 8, 8), 8)]
        return t == d, orb_ref.at[j, 0], dst, in_send.at[j], in_recv, {"dom": t}

    @when(o < 6)
    def _():
        loop(12, lambda i: start(*pot_args(far_first(i))))

    loop(12, lambda i: start(*in_args(far_first(i))))

    def share_args(n):
        q, b = n // 8, n % 8
        return b == o, potb.at[q, o], potb.at[q, o], g_send.at[n], g_recv.at[o], {"orb": b}

    def out_args(at, m):
        q, col = m // 8, m % 8
        src = buf.at[at, pl.ds(RADIUS + q * 6, 6), pl.ds(pl.multiple_of(8 + col * 8, 8), 8)]
        t = c * 32 + m
        return t == d, src, back.at[at, orbital], b_send.at[at, m], b_recv.at[at], {"dom": t}

    @when(active)
    def _():
        @when(o < 6)
        def _():
            def share(i):
                q = (z // 4 + jnp.where(i == 2, 3, jnp.where(i == 3, 2, i))) % 4
                landed(potb.at[q, 0], p_recv.at[q])

                def one(b):
                    here, src, dst, send, recv, axes = share_args(q * 8 + b)

                    @when(jnp.logical_not(here))
                    def _():
                        copy_to(src, dst, send, recv, axes).start()

                loop(8, one)

            loop(4, share)

        def shared(r):
            @when(r != o)
            def _():
                landed(potb.at[:, 0], g_recv.at[r])

        loop(6, shared)
        landed(buf.at[0, pl.ds(RADIUS, ROWS), pl.ds(8, 64)], in_recv)

        def step(s):
            cur, new = (s + 1) % 2, s % 2
            halo = copy_to(
                buf.at[cur, pl.ds(24 - 18 * c, 6), pl.ds(8, 64)],
                buf.at[cur, pl.ds(30 * c, 6), pl.ds(8, 64)],
                h_send.at[cur], h_recv.at[cur], partner,
            )
            halo.start()
            scale, shift, past = scal[3 * s], scal[3 * s + 1], scal[3 * s + 2]

            def block(i):
                @when(i == 3)
                def _():
                    halo.wait_recv()

                blk = jnp.where(c == 0, i, 3 - i)
                r0 = RADIUS + blk * 6
                x = buf[cur, pl.ds(r0, 6), 8:72, :].reshape(6 * 64, 128)
                zs[...] = jnp.dot(x, w[...], precision=HI, preferred_element_type=F32).reshape(6, 64, 128)
                for yt in range(8):
                    y0 = 8 + 8 * yt
                    col = [buf[cur, r0 - RADIUS + m, y0 : y0 + 8, :] for m in range(18)]
                    for i6 in range(6):
                        r = r0 + i6
                        acc = zs[i6, y0 - 8 : y0, :]
                        mid = col[i6 + RADIUS]
                        for k in range(1, RADIUS + 1):
                            term = col[i6 + RADIUS + k] + col[i6 + RADIUS - k]
                            term = term + (
                                buf[cur, r, y0 + k : y0 + k + 8, :] + buf[cur, r, y0 - k : y0 - k + 8, :]
                            )
                            acc = acc + (-0.5 * COEF[k]) * term
                        acc = acc + (potb[blk, i6, y0 - 8 : y0, :] - shift) * mid
                        buf[new, r, y0 : y0 + 8, :] = scale * acc - past * buf[new, r, y0 : y0 + 8, :]

                @when(s >= DEGREE)
                def _():
                    loop(8, lambda col: start(*out_args(new, blk * 8 + col)))

            loop(4, block)
            halo.wait_send()

        loop(DEGREE + 1, lambda s: step(s + 1))

    def meet_args(what, r):
        b = (r + z) % 8
        dst = every.at[what, pl.ds(o * 12, 12)]
        return b == o, back.at[what, :, r], dst, m_send.at[what, r], m_recv.at[what], {"orb": b}

    def send_meet(what):
        landed(back.at[what], b_recv.at[what])
        loop(6, lambda r: start(*meet_args(what, r)))

    def r1_args(what, m):
        axes = {"orb": m % 8, "dom": (m // 8) * 32 + z * 2 + what}
        here = (tile == m) & (c == what)
        return here, gram.at[what, m], r1.at[meet_row * 4 + y_lo * 2 + c], r1_send.at[what, m], r1_recv, axes

    def r2_args(b):
        return b == z, mine.at[0], r2.at[z], r2_send.at[b], r2_recv, {"dom": y_lo * 32 + b * 2 + c}

    def r3_args(n):
        b, y, core = n // 4, (n // 2) % 2, n % 2
        here = (b == o) & (y == y_lo) & (core == c)
        axes = {"orb": b, "dom": y * 32 + z * 2 + core}
        return here, mine.at[1], full.at[c, tile], r3_send.at[n], full_recv.at[c], axes

    def meet_sums(what):
        @when(meets)
        def _():
            landed(every.at[what], m_recv.at[what])
            acc = jnp.zeros((NORB, NORB), F32)
            for s in range(8):
                acc = acc + lax.dot_general(
                    every[0, :, s, :], every[what, :, s, :], (((1,), (1,)), ((), ())),
                    precision=HI, preferred_element_type=F32,
                )
            for m in range(12):
                gram[what, m] = jnp.zeros((8, 128), F32)
                gram[what, m, :, 0:NORB] = acc[8 * m : 8 * m + 8, :]
            loop(12, lambda m: start(*r1_args(what, m)))

    def plane_sum(what):
        @when(owns & (c == what))
        def _():
            landed(r1, r1_recv)
            parts = [r1[b] for b in range(24)]
            while len(parts) > 1:
                parts = [sum(parts[i + 1 : i + 2], parts[i]) for i in range(0, len(parts), 2)]
            mine[0] = parts[0]
            loop(16, lambda b: start(*r2_args(b)))

    def whole_sum(what):
        @when(owns & (c == what))
        def _():
            landed(r2, r2_recv)
            parts = [r2[b] for b in range(16)]
            while len(parts) > 1:
                parts = [parts[i] + parts[i + 1] for i in range(0, len(parts), 2)]
            mine[1] = parts[0] * (1.0 / CELLS)
            loop(32, lambda n: start(*r3_args(n)))

    send_meet(0)
    meet_sums(0)
    send_meet(1)
    plane_sum(0)
    meet_sums(1)
    whole_sum(0)
    plane_sum(1)
    landed(full.at[0], full_recv.at[0])
    inverse = inverse_factor(full[0].reshape(NORB, 128))[:, :NORB]

    def o_args(b):
        dst = out_ref.at[:, 0, meet_row]
        return b == o, rot.at[pl.ds(b * 12, 12)], dst, o_send.at[b], o_recv, {"orb": b}

    @when(meets)
    def _():
        for s in range(8):
            rot[:, s, :] = jnp.dot(inverse, every[0, :, s, :], precision=HI, preferred_element_type=F32)
        loop(8, lambda b: start(*o_args(b)))

    whole_sum(1)
    landed(full.at[1], full_recv.at[1])
    projected = full[1].reshape(NORB, 128)[:, :NORB]
    half = jnp.dot(inverse, projected, precision=HI, preferred_element_type=F32)
    sub_ref[...] = lax.dot_general(
        half, inverse, (((1,), (1,)), ((), ())), precision=HI, preferred_element_type=F32
    )

    loop(12, lambda j: left(*in_args(j)))

    @when(o < 6)
    def _():
        loop(12, lambda j: left(*pot_args(j)))

    @when(active)
    def _():
        @when(o < 6)
        def _():
            loop(32, lambda n: left(*share_args(n)))

        loop(32, lambda m: left(*out_args(0, m)))
        loop(32, lambda m: left(*out_args(1, m)))

    for what in range(2):
        loop(6, lambda r: left(*meet_args(what, r)))

        @when(meets)
        def _():
            loop(12, lambda m: left(*r1_args(what, m)))

    @when(owns)
    def _():
        loop(16, lambda b: left(*r2_args(b)))
        loop(32, lambda n: left(*r3_args(n)))

    @when(meets)
    def _():
        loop(8, lambda b: left(*o_args(b)))

    landed(out_ref, o_recv)


def local(orbitals, potential):
    vmem, anyspace = pl.BlockSpec(memory_space=pltpu.VMEM), pl.BlockSpec(memory_space=pl.ANY)
    dma = pltpu.SemaphoreType.DMA
    return pl.pallas_call(
        kernel,
        out_shape=(
            jax.ShapeDtypeStruct(orbitals.shape, F32),
            jax.ShapeDtypeStruct((NORB, NORB), F32),
        ),
        in_specs=[anyspace, anyspace],
        out_specs=(anyspace, vmem),
        scratch_shapes=[
            pltpu.VMEM((2, EXT_ROWS, EXT_COLS, 128), F32),
            pltpu.VMEM((4, 6, 64, 128), F32),
            pltpu.VMEM((6, 64, 128), F32),
            pltpu.VMEM((128, 128), F32),
            pltpu.SMEM((32,), F32),
            pltpu.VMEM((2, 12, 6, 8, 128), F32),
            pltpu.VMEM((2, NORB, 8, 128), F32),
            pltpu.VMEM((2, 12, 8, 128), F32),
            pltpu.VMEM((24, 8, 128), F32),
            pltpu.VMEM((16, 8, 128), F32),
            pltpu.VMEM((2, 8, 128), F32),
            pltpu.VMEM((2, 12, 8, 128), F32),
            pltpu.VMEM((NORB, 8, 128), F32),
            dma((12,)), dma, dma((12,)), dma((4,)), dma((32,)), dma((6,)), dma((2,)), dma((2,)),
            dma((2, 32)), dma((2,)), dma((2, 6)), dma((2,)),
            dma((2, 12)), dma, dma((16,)), dma, dma((32,)), dma((2,)), dma((8,)), dma,
        ],
        compiler_params=pltpu.CompilerParams(
            collective_id=0, has_side_effects=True, vmem_limit_bytes=60 * 2**20
        ),
        name="filter_and_rotate",
    )(orbitals, potential)


def solution(mesh):
    return jax.shard_map(
        local,
        mesh=mesh,
        in_specs=(P("orb", "dom", None, None, None), P("dom", None, None, None)),
        out_specs=(P("orb", "dom", None, None, None), P()),
        check_vma=False,
    )
```

time: 912 us -> 147 us (0.16)
  waiting for transfers between devices: 705 us -> 0 us
  starting transfers between devices: 147 us -> 0 us
  Pallas kernels: 0 us -> 144 us
  other arithmetic: 31.4 us -> 0 us
  between operations: 14.9 us -> 0.65 us
    psum x1 -> x0, waiting for transfers between devices: 442 us -> none  [local(): over_sum, proj_sum = lax.psum((over_part, proj_part), ('dom', 'orb'))]
    ppermute x36 -> x0, waiting for transfers between devices: 231 us -> none  [from_behind(): lax.ppermute(value, axis, [(source, source + steps) for source in range(i...]
    ppermute x36 -> x0, starting transfers between devices: 147 us -> none  [from_behind(): lax.ppermute(value, axis, [(source, source + steps) for source in range(i...]
    pallas_call x0 -> x1, Pallas kernels: none -> 144 us  [local(): pl.pallas_call(kernel, out_shape=(jax.ShapeDtypeStruct(orbitals.shape, F3...]
    all_gather x1 -> x0, waiting for transfers between devices: 31.5 us -> none  [local(): piece = lax.all_gather(flat_f, 'orb', axis=0, tiled=True)]
    another operation x5 -> x0, other arithmetic: 17.5 us -> none  [the longest x3 9.45 us: local(): lower = jnp.linalg.cholesky(intersection)]
    sub x7 -> x0, other arithmetic: 9.4 us -> none  [local(): (hamiltonian(newer, pot, keep_low, keep_high) - CENTER * newer) * (2.0 *...]
  transfers between devices with their start and end apart: 38 -> 0, of which waited for: 24 -> 0; matrix products, arithmetic and copies ran while one was open for 0% -> 0% of each run, Pallas kernels for 0% -> 0%
where the time goes in v2:
time: 147 us
  Pallas kernels  144 us (98%)
  local copies, waits for them, and re-layouts  2.33 us (2%)
    pallas_call x1, Pallas kernels, local(): pl.pallas_call(kernel, out_shape=(jax.ShapeDtypeStruct(orbitals.shape, F3...  144 us

profile of v2, /device:TPU:1, one launch (start us, length us, event | category | flops | bytes accessed | tf_op | source)
XLA Modules:
  0.0 147.1 jit_solution(13535322475433192565)
XLA Ops:
  0.6 144.2 %filter_and_rotate.1 = (f32[12,1,6,8,128]{4,3,2,1,0:T(8,128)}, f32[96,96]{1,0:T(8,128)}) custom-call(f32[12,1,6,8,128]{4,3,2,1,0:T(8,128)} %orb_ref.1, f32[1,6,8,128]{3,2,1,0:T(8,128)} %pot_ref.1), custom_call_target="tpu_custom_call" | custom-call | tf_op jit(solution)/shard_map/filter_and_rotate/pallas_call | solution.py:416
  144.8 0.0 copy-start
  144.8 1.7 %copy.6 = f32[12,1,6,8,128]{4,3,2,1,0:T(8,128)} copy(f32[12,1,6,8,128]{4,3,2,1,0:T(8,128)} %get-tuple-element.4) | data formatting | bytes 589824
  146.5 0.0 copy-done
  146.5 0.6 copy.7
Async XLA Ops:
  144.8 1.7 %copy-start = (f32[96,96]{1,0:T(8,128)S(1)}, f32[96,96]{1,0:T(8,128)}, u32[]{:S(2)}) copy-start(f32[96,96]{1,0:T(8,128)} %get-tuple-element.5) | copy-start | bytes 110596

commit v3 on v2

--- a/solution.py
+++ b/solution.py
@@ -41,7 +41,7 @@
         rows.append((2.0 * sigma_next / E_HALF, CENTER, sigma * sigma_next))
         sigma = sigma_next
     rows.append((1.0, 0.0, 0.0))
-    return rows
+    return [(scale, center + 1.5 * COEF[0], past) for scale, center, past in rows]
 
 
 def holder(j, c):
@@ -111,8 +111,8 @@
 
 def kernel(
     orb_ref, pot_ref, out_ref, sub_ref,
-    buf, potb, zs, w, scal, back, every, gram, r1, r2, mine, full, rot,
-    in_send, in_recv, p_send, p_recv, g_send, g_recv, h_send, h_recv, b_send, b_recv, m_send, m_recv,
+    buf0, buf1, potb, w, scal, every, gram, r1, r2, mine, full, rot,
+    in_send, in_recv, p_send, p_recv, g_send, g_recv, h_send, h_recv, m_send, m_recv, mates,
     r1_send, r1_recv, r2_send, r2_recv, r3_send, full_recv, o_send, o_recv,
 ):
     d, o = lax.axis_index("dom"), lax.axis_index("orb")
@@ -151,9 +151,12 @@
 
     @when(active)
     def _():
-        loop(32, lambda m: greet(c * 32 + m != d, {"dom": c * 32 + m}))
-
-    loop(12, lambda j: greet(holder(j, y_lo) != d, {"dom": holder(j, y_lo)}))
+        def source(i):
+            m = c * 32 + (2 * z + 16 + jnp.where(i % 2 == 0, 32 - i // 2, (i + 1) // 2)) % 32
+            greet(m != d, {"dom": m})
+
+        loop(32, source)
+
     loop(8, lambda b: greet(b != o, {"orb": b}))
 
     partner = {"dom": d + 1 - 2 * c}
@@ -163,30 +166,34 @@
         margin, side = jnp.zeros((EXT_COLS, 128), F32), jnp.zeros((8, 128), F32)
 
         def clear(i):
-            buf[1, i] = margin
-            buf[0, i, 0:8, :] = side
-            buf[0, i, 72:80, :] = side
+            buf1[i] = margin
+            buf0[i, 0:8, :] = side
+            buf0[i, 72:80, :] = side
 
         loop(EXT_ROWS, clear)
 
         def clear_rows(i):
-            buf[0, i] = margin
-            buf[0, i + EXT_ROWS - RADIUS] = margin
+            buf0[i] = margin
+            buf0[i + EXT_ROWS - RADIUS] = margin
 
         loop(RADIUS, clear_rows)
         gap = jnp.abs(
             lax.broadcasted_iota(jnp.int32, (128, 128), 0) - lax.broadcasted_iota(jnp.int32, (128, 128), 1)
         )
-        weights = jnp.where(gap == 0, -1.5 * COEF[0], 0.0)
+        weights = jnp.zeros((128, 128), F32)
         for k in range(1, RADIUS + 1):
             weights = jnp.where(gap == k, -0.5 * COEF[k], weights)
-        w[...] = weights.astype(F32)
+        high = weights.astype(jnp.bfloat16)
+        low = (weights - high.astype(F32)).astype(jnp.bfloat16)
+        for i in range(2):
+            w[128 * i : 128 * i + 128, 0:128] = high
+            w[128 * i : 128 * i + 128, 128:256] = low
         for s, row in enumerate(step_scalars()):
             for i, value in enumerate(row):
                 scal[3 * s + i] = jnp.float32(value)
         greet(active, partner)
 
-    pl.semaphore_wait(barrier, 19 + 33 * active.astype(jnp.int32) - 2 * selfpair.astype(jnp.int32))
+    pl.semaphore_wait(barrier, 19 + active.astype(jnp.int32) - selfpair.astype(jnp.int32))
 
     far = (((z + 8) % 16) * 3) // 4
     col0 = pl.multiple_of(pcol * 8, 8)
@@ -200,7 +207,7 @@
 
     def in_args(j):
         t = holder(j, y_lo)
-        dst = buf.at[0, pl.ds(RADIUS + (prow % 4) * 6, 6), pl.ds(pl.multiple_of(8 + pcol * 8, 8), 8)]
+        dst = buf0.at[pl.ds(RADIUS + (prow % 4) * 6, 6), pl.ds(pl.multiple_of(8 + pcol * 8, 8), 8)]
         return t == d, orb_ref.at[j, 0], dst, in_send.at[j], in_recv, {"dom": t}
 
     @when(o < 6)
@@ -213,11 +220,12 @@
         q, b = n // 8, n % 8
         return b == o, potb.at[q, o], potb.at[q, o], g_send.at[n], g_recv.at[o], {"orb": b}
 
-    def out_args(at, m):
-        q, col = m // 8, m % 8
-        src = buf.at[at, pl.ds(RADIUS + q * 6, 6), pl.ds(pl.multiple_of(8 + col * 8, 8), 8)]
+    def out_args(what, m, r):
+        src = (buf0, buf1)[what].at[RADIUS + (m // 8) * 6 + r, pl.ds(pl.multiple_of(8 + (m % 8) * 8, 8), 8)]
         t = c * 32 + m
-        return t == d, src, back.at[at, orbital], b_send.at[at, m], b_recv.at[at], {"dom": t}
+        b = (r + m // 2) % 8
+        axes = {"orb": b, "dom": t}
+        return (t == d) & (b == o), src, every.at[what, o * 12 + orbital], m_send.at[what, m], m_recv.at[what], axes
 
     @when(active)
     def _():
@@ -244,17 +252,29 @@
                 landed(potb.at[:, 0], g_recv.at[r])
 
         loop(6, shared)
-        landed(buf.at[0, pl.ds(RADIUS, ROWS), pl.ds(8, 64)], in_recv)
-
-        def step(s):
-            cur, new = (s + 1) % 2, s % 2
+        landed(buf0.at[pl.ds(RADIUS, ROWS), pl.ds(8, 64)], in_recv)
+
+        def tell(b):
+            @when(b != o)
+            def _():
+                pl.semaphore_signal(mates, inc=1, device_id={"orb": b}, device_id_type=MESH)
+
+        loop(8, tell)
+
+        def step(s, what, cur, new, send):
             halo = copy_to(
-                buf.at[cur, pl.ds(24 - 18 * c, 6), pl.ds(8, 64)],
-                buf.at[cur, pl.ds(30 * c, 6), pl.ds(8, 64)],
-                h_send.at[cur], h_recv.at[cur], partner,
+                cur.at[pl.ds(24 - 18 * c, 6), pl.ds(8, 64)],
+                cur.at[pl.ds(30 * c, 6), pl.ds(8, 64)],
+                h_send.at[what], h_recv.at[what], partner,
             )
             halo.start()
             scale, shift, past = scal[3 * s], scal[3 * s + 1], scal[3 * s + 2]
+            x = cur[RADIUS : RADIUS + ROWS, 8:72, :].reshape(ROWS * 64, 128)
+            high = x.astype(jnp.bfloat16)
+            low = (x - high.astype(F32)).astype(jnp.bfloat16)
+            along = jnp.dot(jnp.concatenate([high, low], axis=1), w[...], preferred_element_type=F32)
+            along = (along[:, :128] + along[:, 128:]).reshape(ROWS, 64, 128)
+            new[RADIUS : RADIUS + ROWS, 8:72, :] = scale * along - past * new[RADIUS : RADIUS + ROWS, 8:72, :]
 
             def block(i):
                 @when(i == 3)
@@ -263,41 +283,41 @@
 
                 blk = jnp.where(c == 0, i, 3 - i)
                 r0 = RADIUS + blk * 6
-                x = buf[cur, pl.ds(r0, 6), 8:72, :].reshape(6 * 64, 128)
-                zs[...] = jnp.dot(x, w[...], precision=HI, preferred_element_type=F32).reshape(6, 64, 128)
                 for yt in range(8):
                     y0 = 8 + 8 * yt
-                    col = [buf[cur, r0 - RADIUS + m, y0 : y0 + 8, :] for m in range(18)]
+                    col = [cur[r0 - RADIUS + m, y0 : y0 + 8, :] for m in range(18)]
                     for i6 in range(6):
                         r = r0 + i6
-                        acc = zs[i6, y0 - 8 : y0, :]
                         mid = col[i6 + RADIUS]
+                        acc = (potb[blk, i6, y0 - 8 : y0, :] - shift) * mid
                         for k in range(1, RADIUS + 1):
                             term = col[i6 + RADIUS + k] + col[i6 + RADIUS - k]
-                            term = term + (
-                                buf[cur, r, y0 + k : y0 + k + 8, :] + buf[cur, r, y0 - k : y0 - k + 8, :]
-                            )
+                            term = term + (cur[r, y0 + k : y0 + k + 8, :] + cur[r, y0 - k : y0 - k + 8, :])
                             acc = acc + (-0.5 * COEF[k]) * term
-                        acc = acc + (potb[blk, i6, y0 - 8 : y0, :] - shift) * mid
-                        buf[new, r, y0 : y0 + 8, :] = scale * acc - past * buf[new, r, y0 : y0 + 8, :]
-
-                @when(s >= DEGREE)
+                        new[r, y0 : y0 + 8, :] = scale * acc + new[r, y0 : y0 + 8, :]
+
+                @when(send)
                 def _():
-                    loop(8, lambda col: start(*out_args(new, blk * 8 + col)))
+                    def row(n):
+                        start(*out_args(1 - what, blk * 8 + n // 6, n % 6))
+
+                    loop(48, row)
 
             loop(4, block)
             halo.wait_send()
 
-        loop(DEGREE + 1, lambda s: step(s + 1))
-
-    def meet_args(what, r):
-        b = (r + z) % 8
-        dst = every.at[what, pl.ds(o * 12, 12)]
-        return b == o, back.at[what, :, r], dst, m_send.at[what, r], m_recv.at[what], {"orb": b}
-
-    def send_meet(what):
-        landed(back.at[what], b_recv.at[what])
-        loop(6, lambda r: start(*meet_args(what, r)))
+        def two_steps(i):
+            step(2 * i + 1, 0, buf0, buf1, i == 4)
+
+            @when(i < 4)
+            def _():
+                @when(i == 3)
+                def _():
+                    pl.semaphore_wait(mates, 7)
+
+                step(2 * i + 2, 1, buf1, buf0, i == 3)
+
+        loop(5, two_steps)
 
     def r1_args(what, m):
         axes = {"orb": m % 8, "dom": (m // 8) * 32 + z * 2 + what}
@@ -348,9 +368,7 @@
             mine[1] = parts[0] * (1.0 / CELLS)
             loop(32, lambda n: start(*r3_args(n)))
 
-    send_meet(0)
     meet_sums(0)
-    send_meet(1)
     plane_sum(0)
     meet_sums(1)
     whole_sum(0)
@@ -388,11 +406,21 @@
         def _():
             loop(32, lambda n: left(*share_args(n)))
 
-        loop(32, lambda m: left(*out_args(0, m)))
-        loop(32, lambda m: left(*out_args(1, m)))
+        for what in range(2):
+            def gone(m):
+                alone = (c * 32 + m == d) & meets
+
+                @when(alone)
+                def _():
+                    landed(every.at[what, pl.ds(0, 5)], m_send.at[what, m])
+
+                @when(jnp.logical_not(alone))
+                def _():
+                    landed(every.at[what, pl.ds(0, 6)], m_send.at[what, m])
+
+            loop(32, gone)
 
     for what in range(2):
-        loop(6, lambda r: left(*meet_args(what, r)))
 
         @when(meets)
         def _():
@@ -422,12 +450,11 @@
         in_specs=[anyspace, anyspace],
         out_specs=(anyspace, vmem),
         scratch_shapes=[
-            pltpu.VMEM((2, EXT_ROWS, EXT_COLS, 128), F32),
+            pltpu.VMEM((EXT_ROWS, EXT_COLS, 128), F32),
+            pltpu.VMEM((EXT_ROWS, EXT_COLS, 128), F32),
             pltpu.VMEM((4, 6, 64, 128), F32),
-            pltpu.VMEM((6, 64, 128), F32),
-            pltpu.VMEM((128, 128), F32),
+            pltpu.VMEM((256, 256), jnp.bfloat16),
             pltpu.SMEM((32,), F32),
-            pltpu.VMEM((2, 12, 6, 8, 128), F32),
             pltpu.VMEM((2, NORB, 8, 128), F32),
             pltpu.VMEM((2, 12, 8, 128), F32),
             pltpu.VMEM((24, 8, 128), F32),
@@ -436,7 +463,7 @@
             pltpu.VMEM((2, 12, 8, 128), F32),
             pltpu.VMEM((NORB, 8, 128), F32),
             dma((12,)), dma, dma((12,)), dma((4,)), dma((32,)), dma((6,)), dma((2,)), dma((2,)),
-            dma((2, 32)), dma((2,)), dma((2, 6)), dma((2,)),
+            dma((2, 32)), dma((2,)), pltpu.SemaphoreType.REGULAR,
             dma((2, 12)), dma, dma((16,)), dma, dma((32,)), dma((2,)), dma((8,)), dma,
         ],
         compiler_params=pltpu.CompilerParams(

time: 147 us -> 127 us (0.86)
  Pallas kernels: 144 us -> 124 us
    pallas_call x1, Pallas kernels: 144 us -> 124 us  [local(): pl.pallas_call(kernel, out_shape=(jax.ShapeDtypeStruct(orbitals.shape, F3...]
where the time goes in v3:
time: 127 us
  Pallas kernels  124 us (98%)
  local copies, waits for them, and re-layouts  2.33 us (2%)
    pallas_call x1, Pallas kernels, local(): pl.pallas_call(kernel, out_shape=(jax.ShapeDtypeStruct(orbitals.shape, F3...  124 us

profile of v3, /device:TPU:1, one launch (start us, length us, event | category | flops | bytes accessed | tf_op | source)
XLA Modules:
  0.0 126.8 jit_solution(9771613808470271426)
XLA Ops:
  0.6 123.9 %filter_and_rotate.1 = (f32[12,1,6,8,128]{4,3,2,1,0:T(8,128)}, f32[96,96]{1,0:T(8,128)}) custom-call(f32[12,1,6,8,128]{4,3,2,1,0:T(8,128)} %orb_ref.1, f32[1,6,8,128]{3,2,1,0:T(8,128)} %pot_ref.1), custom_call_target="tpu_custom_call" | custom-call | tf_op jit(solution)/shard_map/filter_and_rotate/pallas_call | solution.py:444
  124.5 0.0 copy-start
  124.5 1.7 %copy.6 = f32[12,1,6,8,128]{4,3,2,1,0:T(8,128)} copy(f32[12,1,6,8,128]{4,3,2,1,0:T(8,128)} %get-tuple-element.4) | data formatting | bytes 589824
  126.2 0.0 copy-done
  126.2 0.6 copy.7
Async XLA Ops:
  124.5 1.7 %copy-start = (f32[96,96]{1,0:T(8,128)S(1)}, f32[96,96]{1,0:T(8,128)}, u32[]{:S(2)}) copy-start(f32[96,96]{1,0:T(8,128)} %get-tuple-element.5) | copy-start | bytes 110596

commit v4 on v3

--- a/solution.py
+++ b/solution.py
@@ -31,6 +31,8 @@
 EXT_ROWS = ROWS + 2 * RADIUS
 EXT_COLS = 80
 
+PAUSE = 92
+
 
 def step_scalars():
     rows = [(0.0, 0.0, 0.0)]
@@ -75,45 +77,64 @@
     return jnp.broadcast_to(tile[r : r + 1, :], (8, 128))
 
 
-def inverse_factor(matrix):
+def inverse_factor(matrix, pause_at, pause):
+    wide = 4
     sub = lax.broadcasted_iota(jnp.int32, (8, 128), 0)
     lane = lax.broadcasted_iota(jnp.int32, (8, 128), 1)
     tiles = NORB // 8
     st = [matrix[8 * t : 8 * t + 8, :] for t in range(tiles)]
     et = [jnp.where(lane == sub + 8 * t, 1.0, 0.0).astype(F32) for t in range(tiles)]
-    for j in range(0, NORB, 2):
+    for j in range(0, NORB, wide):
+        if j == pause_at:
+            pause()
         t0, r = divmod(j, 8)
-        c0 = [over_lanes(st[t], j) for t in range(t0, tiles)]
-        c1 = [over_lanes(st[t], j + 1) for t in range(t0, tiles)]
-        a, b, c = over_rows(c0[0], r), over_rows(c0[0], r + 1), over_rows(c1[0], r + 1)
-        s0, s1 = over_rows(st[t0], r), over_rows(st[t0], r + 1)
-        e0, e1 = over_rows(et[t0], r), over_rows(et[t0], r + 1)
-        inv_a = 1.0 / a
-        q = b * inv_a
-        d = c - b * q
-        inv_d = 1.0 / d
-        s1 = (s1 - q * s0) * inv_d
-        e1 = e1 - q * e0
-        s0 = s0 * inv_a
-        e0d, e1d = e0 * inv_a, e1 * inv_d
+        cols = [[over_lanes(st[t], j + k) for k in range(wide)] for t in range(t0, tiles)]
+        a = {(k, q): over_rows(cols[0][q], r + k) for k in range(wide) for q in range(k + 1)}
+        inv, low = [], {}
+        for p in range(wide):
+            inv.append(1.0 / a[p, p])
+            for k in range(p + 1, wide):
+                low[k, p] = a[k, p] * inv[p]
+            for k in range(p + 1, wide):
+                for q in range(p + 1, k + 1):
+                    a[k, q] = a[k, q] - low[k, p] * a[q, p]
+
+        def forward(rows):
+            done = []
+            for k, row in enumerate(rows):
+                for p in range(k):
+                    row = row - low[k, p] * done[p]
+                done.append(row)
+            return done
+
+        srow = forward([over_rows(st[t0], r + k) for k in range(wide)])
+        erow = forward([over_rows(et[t0], r + k) for k in range(wide)])
+        sdiv = [row * i for row, i in zip(srow, inv)]
+        ediv = [row * i for row, i in zip(erow, inv)]
         for t in range(t0, tiles):
-            m0 = c0[t - t0]
-            m1 = c1[t - t0] - m0 * q
+            if t == t0 and r + wide == 8:
+                continue
+            mult = []
+            for k in range(wide):
+                col = cols[t - t0][k]
+                for p in range(k):
+                    col = col - mult[p] * low[k, p]
+                mult.append(col)
             if t == t0:
-                m0, m1 = jnp.where(sub > r + 1, m0, 0.0), jnp.where(sub > r + 1, m1, 0.0)
-            st[t] = st[t] - m0 * s0 - m1 * s1
-            et[t] = et[t] - m0 * e0d - m1 * e1d
-        et[t0] = jnp.where(
-            sub == r, e0 * lax.rsqrt(a), jnp.where(sub == r + 1, e1 * lax.rsqrt(d), et[t0])
-        )
+                mult = [jnp.where(sub >= r + wide, col, 0.0) for col in mult]
+            for k in range(wide):
+                st[t] = st[t] - mult[k] * sdiv[k]
+                et[t] = et[t] - mult[k] * ediv[k]
+        for k in range(wide):
+            et[t0] = jnp.where(sub == r + k, erow[k] * lax.rsqrt(a[k, k]), et[t0])
     return jnp.concatenate(et, axis=0)
 
 
 def kernel(
     orb_ref, pot_ref, out_ref, sub_ref,
-    buf0, buf1, potb, w, scal, every, gram, r1, r2, mine, full, rot,
+    buf0, buf1, potb, w, scal, every, gram, r1, r2, mine, full, rot, sub,
     in_send, in_recv, p_send, p_recv, g_send, g_recv, h_send, h_recv, m_send, m_recv, mates,
-    r1_send, r1_recv, r2_send, r2_recv, r3_send, full_recv, o_send, o_recv,
+    r1_send, r1_recv, r2_send, r2_recv, r3_send, full_recv, o_send, o_recv, sub_sem,
 ):
     d, o = lax.axis_index("dom"), lax.axis_index("orb")
     y_lo, z, c = d // 32, (d // 2) % 16, d % 2
@@ -184,10 +205,12 @@
         for k in range(1, RADIUS + 1):
             weights = jnp.where(gap == k, -0.5 * COEF[k], weights)
         high = weights.astype(jnp.bfloat16)
-        low = (weights - high.astype(F32)).astype(jnp.bfloat16)
-        for i in range(2):
-            w[128 * i : 128 * i + 128, 0:128] = high
-            w[128 * i : 128 * i + 128, 128:256] = low
+        rest = weights - high.astype(F32)
+        middle = rest.astype(jnp.bfloat16)
+        low = (rest - middle.astype(F32)).astype(jnp.bfloat16)
+        for i, row in enumerate(((high, middle, high), (high, middle, low))):
+            for n, part in enumerate(row):
+                w[128 * i : 128 * i + 128, 128 * n : 128 * n + 128] = part
         for s, row in enumerate(step_scalars()):
             for i, value in enumerate(row):
                 scal[3 * s + i] = jnp.float32(value)
@@ -214,7 +237,13 @@
     def _():
         loop(12, lambda i: start(*pot_args(far_first(i))))
 
-    loop(12, lambda i: start(*in_args(far_first(i))))
+    def send_in():
+        loop(12, lambda i: start(*in_args(far_first(i))))
+
+    @when(jnp.logical_not(active))
+    def _():
+        send_in()
+
 
     def share_args(n):
         q, b = n // 8, n % 8
@@ -227,6 +256,20 @@
         axes = {"orb": b, "dom": t}
         return (t == d) & (b == o), src, every.at[what, o * 12 + orbital], m_send.at[what, m], m_recv.at[what], axes
 
+    def gone(what):
+        def one(m):
+            alone = (c * 32 + m == d) & meets
+
+            @when(alone)
+            def _():
+                landed(every.at[what, pl.ds(0, 5)], m_send.at[what, m])
+
+            @when(jnp.logical_not(alone))
+            def _():
+                landed(every.at[what, pl.ds(0, 6)], m_send.at[what, m])
+
+        loop(32, one)
+
     @when(active)
     def _():
         @when(o < 6)
@@ -245,6 +288,8 @@
                 loop(8, one)
 
             loop(4, share)
+
+        send_in()
 
         def shared(r):
             @when(r != o)
@@ -271,9 +316,12 @@
             scale, shift, past = scal[3 * s], scal[3 * s + 1], scal[3 * s + 2]
             x = cur[RADIUS : RADIUS + ROWS, 8:72, :].reshape(ROWS * 64, 128)
             high = x.astype(jnp.bfloat16)
-            low = (x - high.astype(F32)).astype(jnp.bfloat16)
-            along = jnp.dot(jnp.concatenate([high, low], axis=1), w[...], preferred_element_type=F32)
-            along = (along[:, :128] + along[:, 128:]).reshape(ROWS, 64, 128)
+            rest = x - high.astype(F32)
+            middle = rest.astype(jnp.bfloat16)
+            low = (rest - middle.astype(F32)).astype(jnp.bfloat16)
+            most = jnp.dot(jnp.concatenate([high, middle], axis=1), w[:, :256], preferred_element_type=F32)
+            small = jnp.dot(jnp.concatenate([low, high], axis=1), w[:, 256:], preferred_element_type=F32)
+            along = ((most[:, 128:] + small) + most[:, :128]).reshape(ROWS, 64, 128)
             new[RADIUS : RADIUS + ROWS, 8:72, :] = scale * along - past * new[RADIUS : RADIUS + ROWS, 8:72, :]
 
             def block(i):
@@ -296,18 +344,17 @@
                             acc = acc + (-0.5 * COEF[k]) * term
                         new[r, y0 : y0 + 8, :] = scale * acc + new[r, y0 : y0 + 8, :]
 
-                @when(send)
-                def _():
-                    def row(n):
-                        start(*out_args(1 - what, blk * 8 + n // 6, n % 6))
-
-                    loop(48, row)
+                if send is not False:
+
+                    @when(send)
+                    def _():
+                        loop(48, lambda n: start(*out_args(0, blk * 8 + n // 6, n % 6)))
 
             loop(4, block)
             halo.wait_send()
 
         def two_steps(i):
-            step(2 * i + 1, 0, buf0, buf1, i == 4)
+            step(2 * i + 1, 0, buf0, buf1, False)
 
             @when(i < 4)
             def _():
@@ -318,6 +365,8 @@
                 step(2 * i + 2, 1, buf1, buf0, i == 3)
 
         loop(5, two_steps)
+        gone(0)
+        loop(192, lambda n: start(*out_args(1, n // 6, n % 6)))
 
     def r1_args(what, m):
         axes = {"orb": m % 8, "dom": (m // 8) * 32 + z * 2 + what}
@@ -374,7 +423,7 @@
     whole_sum(0)
     plane_sum(1)
     landed(full.at[0], full_recv.at[0])
-    inverse = inverse_factor(full[0].reshape(NORB, 128))[:, :NORB]
+    inverse = inverse_factor(full[0].reshape(NORB, 128), PAUSE, lambda: whole_sum(1))[:, :NORB]
 
     def o_args(b):
         dst = out_ref.at[:, 0, meet_row]
@@ -386,45 +435,34 @@
             rot[:, s, :] = jnp.dot(inverse, every[0, :, s, :], precision=HI, preferred_element_type=F32)
         loop(8, lambda b: start(*o_args(b)))
 
-    whole_sum(1)
+    loop(12, lambda j: left(*in_args(j)))
+
+    @when(o < 6)
+    def _():
+        loop(12, lambda j: left(*pot_args(j)))
+
+    @when(active)
+    def _():
+        @when(o < 6)
+        def _():
+            loop(32, lambda n: left(*share_args(n)))
+
+        gone(1)
+
+    for what in range(2):
+
+        @when(meets)
+        def _():
+            loop(12, lambda m: left(*r1_args(what, m)))
+
     landed(full.at[1], full_recv.at[1])
     projected = full[1].reshape(NORB, 128)[:, :NORB]
     half = jnp.dot(inverse, projected, precision=HI, preferred_element_type=F32)
-    sub_ref[...] = lax.dot_general(
+    sub[...] = lax.dot_general(
         half, inverse, (((1,), (1,)), ((), ())), precision=HI, preferred_element_type=F32
     )
-
-    loop(12, lambda j: left(*in_args(j)))
-
-    @when(o < 6)
-    def _():
-        loop(12, lambda j: left(*pot_args(j)))
-
-    @when(active)
-    def _():
-        @when(o < 6)
-        def _():
-            loop(32, lambda n: left(*share_args(n)))
-
-        for what in range(2):
-            def gone(m):
-                alone = (c * 32 + m == d) & meets
-
-                @when(alone)
-                def _():
-                    landed(every.at[what, pl.ds(0, 5)], m_send.at[what, m])
-
-                @when(jnp.logical_not(alone))
-                def _():
-                    landed(every.at[what, pl.ds(0, 6)], m_send.at[what, m])
-
-            loop(32, gone)
-
-    for what in range(2):
-
-        @when(meets)
-        def _():
-            loop(12, lambda m: left(*r1_args(what, m)))
+    give = pltpu.make_async_copy(sub, sub_ref, sub_sem)
+    give.start()
 
     @when(owns)
     def _():
@@ -436,10 +474,11 @@
         loop(8, lambda b: left(*o_args(b)))
 
     landed(out_ref, o_recv)
+    give.wait()
 
 
 def local(orbitals, potential):
-    vmem, anyspace = pl.BlockSpec(memory_space=pltpu.VMEM), pl.BlockSpec(memory_space=pl.ANY)
+    anyspace = pl.BlockSpec(memory_space=pl.ANY)
     dma = pltpu.SemaphoreType.DMA
     return pl.pallas_call(
         kernel,
@@ -448,12 +487,12 @@
             jax.ShapeDtypeStruct((NORB, NORB), F32),
         ),
         in_specs=[anyspace, anyspace],
-        out_specs=(anyspace, vmem),
+        out_specs=(anyspace, anyspace),
         scratch_shapes=[
             pltpu.VMEM((EXT_ROWS, EXT_COLS, 128), F32),
             pltpu.VMEM((EXT_ROWS, EXT_COLS, 128), F32),
             pltpu.VMEM((4, 6, 64, 128), F32),
-            pltpu.VMEM((256, 256), jnp.bfloat16),
+            pltpu.VMEM((256, 384), jnp.bfloat16),
             pltpu.SMEM((32,), F32),
             pltpu.VMEM((2, NORB, 8, 128), F32),
             pltpu.VMEM((2, 12, 8, 128), F32),
@@ -462,9 +501,10 @@
             pltpu.VMEM((2, 8, 128), F32),
             pltpu.VMEM((2, 12, 8, 128), F32),
             pltpu.VMEM((NORB, 8, 128), F32),
+            pltpu.VMEM((NORB, NORB), F32),
             dma((12,)), dma, dma((12,)), dma((4,)), dma((32,)), dma((6,)), dma((2,)), dma((2,)),
             dma((2, 32)), dma((2,)), pltpu.SemaphoreType.REGULAR,
-            dma((2, 12)), dma, dma((16,)), dma, dma((32,)), dma((2,)), dma((8,)), dma,
+            dma((2, 12)), dma, dma((16,)), dma, dma((32,)), dma((2,)), dma((8,)), dma, dma,
         ],
         compiler_params=pltpu.CompilerParams(
             collective_id=0, has_side_effects=True, vmem_limit_bytes=60 * 2**20

time: 127 us -> 118 us (0.929)
  Pallas kernels: 124 us -> 115 us
    pallas_call x1, Pallas kernels: 124 us -> 115 us  [local(): pl.pallas_call(kernel, out_shape=(jax.ShapeDtypeStruct(orbitals.shape, F3...]
where the time goes in v4:
time: 118 us
  Pallas kernels  115 us (97%)
  local copies, waits for them, and re-layouts  2.33 us (2%)
    pallas_call x1, Pallas kernels, local(): pl.pallas_call(kernel, out_shape=(jax.ShapeDtypeStruct(orbitals.shape, F3...  115 us

profile of v4, /device:TPU:1, one launch (start us, length us, event | category | flops | bytes accessed | tf_op | source)
XLA Modules:
  0.0 118.1 jit_solution(14434734280431200462)
XLA Ops:
  0.6 115.1 %filter_and_rotate.1 = (f32[12,1,6,8,128]{4,3,2,1,0:T(8,128)}, f32[96,96]{1,0:T(8,128)}) custom-call(f32[12,1,6,8,128]{4,3,2,1,0:T(8,128)} %orb_ref.1, f32[1,6,8,128]{3,2,1,0:T(8,128)} %pot_ref.1), custom_call_target="tpu_custom_call" | custom-call | tf_op jit(solution)/shard_map/filter_and_rotate/pallas_call | solution.py:483
  115.7 0.0 copy-start
  115.8 1.7 %copy.6 = f32[12,1,6,8,128]{4,3,2,1,0:T(8,128)} copy(f32[12,1,6,8,128]{4,3,2,1,0:T(8,128)} %get-tuple-element.4) | data formatting | bytes 589824
  117.5 0.0 copy-done
  117.5 0.6 copy.7
Async XLA Ops:
  115.7 1.7 %copy-start = (f32[96,96]{1,0:T(8,128)S(1)}, f32[96,96]{1,0:T(8,128)}, u32[]{:S(2)}) copy-start(f32[96,96]{1,0:T(8,128)} %get-tuple-element.5) | copy-start | bytes 110596

commit v5 on v4

--- a/solution.py
+++ b/solution.py
@@ -31,8 +31,6 @@
 EXT_ROWS = ROWS + 2 * RADIUS
 EXT_COLS = 80
 
-PAUSE = 92
-
 
 def step_scalars():
     rows = [(0.0, 0.0, 0.0)]
@@ -77,7 +75,7 @@
     return jnp.broadcast_to(tile[r : r + 1, :], (8, 128))
 
 
-def inverse_factor(matrix, pause_at, pause):
+def inverse_factor(matrix):
     wide = 4
     sub = lax.broadcasted_iota(jnp.int32, (8, 128), 0)
     lane = lax.broadcasted_iota(jnp.int32, (8, 128), 1)
@@ -85,8 +83,6 @@
     st = [matrix[8 * t : 8 * t + 8, :] for t in range(tiles)]
     et = [jnp.where(lane == sub + 8 * t, 1.0, 0.0).astype(F32) for t in range(tiles)]
     for j in range(0, NORB, wide):
-        if j == pause_at:
-            pause()
         t0, r = divmod(j, 8)
         cols = [[over_lanes(st[t], j + k) for k in range(wide)] for t in range(t0, tiles)]
         a = {(k, q): over_rows(cols[0][q], r + k) for k in range(wide) for q in range(k + 1)}
@@ -149,6 +145,9 @@
     tile = y_lo * 8 + o
     owns = tile < 12
 
+    def far_pencil(i):
+        return (2 * z + 17 + jnp.where(i % 2 == 0, 32 - i // 2, (i + 1) // 2)) % 32
+
     barrier = pltpu.get_barrier_semaphore()
 
     def greet(cond, axes):
@@ -173,7 +172,7 @@
     @when(active)
     def _():
         def source(i):
-            m = c * 32 + (2 * z + 16 + jnp.where(i % 2 == 0, 32 - i // 2, (i + 1) // 2)) % 32
+            m = c * 32 + far_pencil(i)
             greet(m != d, {"dom": m})
 
         loop(32, source)
@@ -256,8 +255,9 @@
         axes = {"orb": b, "dom": t}
         return (t == d) & (b == o), src, every.at[what, o * 12 + orbital], m_send.at[what, m], m_recv.at[what], axes
 
-    def gone(what):
-        def one(m):
+    def gone(what, first, count):
+        def one(i):
+            m = far_pencil(first + i)
             alone = (c * 32 + m == d) & meets
 
             @when(alone)
@@ -268,7 +268,7 @@
             def _():
                 landed(every.at[what, pl.ds(0, 6)], m_send.at[what, m])
 
-        loop(32, one)
+        loop(count, one)
 
     @when(active)
     def _():
@@ -306,7 +306,7 @@
 
         loop(8, tell)
 
-        def step(s, what, cur, new, send):
+        def step(s, what, cur, new):
             halo = copy_to(
                 cur.at[pl.ds(24 - 18 * c, 6), pl.ds(8, 64)],
                 cur.at[pl.ds(30 * c, 6), pl.ds(8, 64)],
@@ -344,29 +344,24 @@
                             acc = acc + (-0.5 * COEF[k]) * term
                         new[r, y0 : y0 + 8, :] = scale * acc + new[r, y0 : y0 + 8, :]
 
-                if send is not False:
-
-                    @when(send)
-                    def _():
-                        loop(48, lambda n: start(*out_args(0, blk * 8 + n // 6, n % 6)))
-
             loop(4, block)
             halo.wait_send()
 
         def two_steps(i):
-            step(2 * i + 1, 0, buf0, buf1, False)
+            step(2 * i + 1, 0, buf0, buf1)
 
             @when(i < 4)
             def _():
-                @when(i == 3)
-                def _():
-                    pl.semaphore_wait(mates, 7)
-
-                step(2 * i + 2, 1, buf1, buf0, i == 3)
+                step(2 * i + 2, 1, buf1, buf0)
+
+            @when(i == 3)
+            def _():
+                pl.semaphore_wait(mates, 7)
+                loop(192, lambda n: start(*out_args(0, far_pencil(n // 6), n % 6)))
 
         loop(5, two_steps)
-        gone(0)
-        loop(192, lambda n: start(*out_args(1, n // 6, n % 6)))
+        gone(0, 0, 28)
+        loop(192, lambda n: start(*out_args(1, far_pencil(n // 6), n % 6)))
 
     def r1_args(what, m):
         axes = {"orb": m % 8, "dom": (m // 8) * 32 + z * 2 + what}
@@ -423,7 +418,7 @@
     whole_sum(0)
     plane_sum(1)
     landed(full.at[0], full_recv.at[0])
-    inverse = inverse_factor(full[0].reshape(NORB, 128), PAUSE, lambda: whole_sum(1))[:, :NORB]
+    inverse = inverse_factor(full[0].reshape(NORB, 128))[:, :NORB]
 
     def o_args(b):
         dst = out_ref.at[:, 0, meet_row]
@@ -435,6 +430,8 @@
             rot[:, s, :] = jnp.dot(inverse, every[0, :, s, :], precision=HI, preferred_element_type=F32)
         loop(8, lambda b: start(*o_args(b)))
 
+    whole_sum(1)
+
     loop(12, lambda j: left(*in_args(j)))
 
     @when(o < 6)
@@ -447,7 +444,8 @@
         def _():
             loop(32, lambda n: left(*share_args(n)))
 
-        gone(1)
+        gone(0, 28, 4)
+        gone(1, 0, 32)
 
     for what in range(2):
 

time: 118 us -> 115 us (0.975)
  Pallas kernels: 115 us -> 112 us
    pallas_call x1, Pallas kernels: 115 us -> 112 us  [local(): pl.pallas_call(kernel, out_shape=(jax.ShapeDtypeStruct(orbitals.shape, F3...]
where the time goes in v5:
time: 115 us
  Pallas kernels  112 us (97%)
  local copies, waits for them, and re-layouts  2.33 us (2%)
    pallas_call x1, Pallas kernels, local(): pl.pallas_call(kernel, out_shape=(jax.ShapeDtypeStruct(orbitals.shape, F3...  112 us
    unnamed x4, local copies, waits for them, and re-layouts  2.33 us

profile of v5, /device:TPU:1, one launch (start us, length us, event | category | flops | bytes accessed | tf_op | source)
XLA Modules:
  0.0 115.3 jit_solution(6558881248631826112)
XLA Ops:
  0.6 112.4 %filter_and_rotate.1 = (f32[12,1,6,8,128]{4,3,2,1,0:T(8,128)}, f32[96,96]{1,0:T(8,128)}) custom-call(f32[12,1,6,8,128]{4,3,2,1,0:T(8,128)} %orb_ref.1, f32[1,6,8,128]{3,2,1,0:T(8,128)} %pot_ref.1), custom_call_target="tpu_custom_call" | custom-call | tf_op jit(solution)/shard_map/filter_and_rotate/pallas_call | solution.py:481
  113.0 0.0 copy-start
  113.0 1.7 %copy.6 = f32[12,1,6,8,128]{4,3,2,1,0:T(8,128)} copy(f32[12,1,6,8,128]{4,3,2,1,0:T(8,128)} %get-tuple-element.4) | data formatting | bytes 589824
  114.7 0.0 copy-done
  114.7 0.6 copy.7
Async XLA Ops:
  113.0 1.7 %copy-start = (f32[96,96]{1,0:T(8,128)S(1)}, f32[96,96]{1,0:T(8,128)}, u32[]{:S(2)}) copy-start(f32[96,96]{1,0:T(8,128)} %get-tuple-element.5) | copy-start | bytes 110596

commit v6 on v5

--- a/solution.py
+++ b/solution.py
@@ -128,7 +128,7 @@
 
 def kernel(
     orb_ref, pot_ref, out_ref, sub_ref,
-    buf0, buf1, potb, w, scal, every, gram, r1, r2, mine, full, rot, sub,
+    buf0, buf1, potb, w, scal, every, gram, r1, r2, mine, full, rot, inv, sub,
     in_send, in_recv, p_send, p_recv, g_send, g_recv, h_send, h_recv, m_send, m_recv, mates,
     r1_send, r1_recv, r2_send, r2_recv, r3_send, full_recv, o_send, o_recv, sub_sem,
 ):
@@ -147,6 +147,11 @@
 
     def far_pencil(i):
         return (2 * z + 17 + jnp.where(i % 2 == 0, 32 - i // 2, (i + 1) // 2)) % 32
+
+    def far_group(i):
+        across = (i < 3) | (i == 4)
+        along = jnp.where((i == 0) | (i == 3), 2, jnp.where((i == 1) | (i == 5), 1, jnp.where((i == 2) | (i == 6), 3, 0)))
+        return ((o // 4 + across.astype(jnp.int32)) % 2) * 4 + (o % 4 + along) % 4
 
     barrier = pltpu.get_barrier_semaphore()
 
@@ -236,12 +241,12 @@
     def _():
         loop(12, lambda i: start(*pot_args(far_first(i))))
 
-    def send_in():
-        loop(12, lambda i: start(*in_args(far_first(i))))
+    def send_in(first, count):
+        loop(count, lambda i: start(*in_args(far_first(first + i))))
 
     @when(jnp.logical_not(active))
     def _():
-        send_in()
+        send_in(0, 12)
 
 
     def share_args(n):
@@ -272,14 +277,14 @@
 
     @when(active)
     def _():
-        @when(o < 6)
-        def _():
-            def share(i):
+        def share(first, count):
+            def part(n):
+                i = first + n
                 q = (z // 4 + jnp.where(i == 2, 3, jnp.where(i == 3, 2, i))) % 4
                 landed(potb.at[q, 0], p_recv.at[q])
 
                 def one(b):
-                    here, src, dst, send, recv, axes = share_args(q * 8 + b)
+                    here, src, dst, send, recv, axes = share_args(q * 8 + far_group(b))
 
                     @when(jnp.logical_not(here))
                     def _():
@@ -287,9 +292,16 @@
 
                 loop(8, one)
 
-            loop(4, share)
-
-        send_in()
+            @when(o < 6)
+            def _():
+                loop(count, part)
+
+        share(0, 2)
+        send_in(0, 4)
+        share(2, 1)
+        send_in(4, 4)
+        share(3, 1)
+        send_in(8, 4)
 
         def shared(r):
             @when(r != o)
@@ -400,7 +412,7 @@
             while len(parts) > 1:
                 parts = [sum(parts[i + 1 : i + 2], parts[i]) for i in range(0, len(parts), 2)]
             mine[0] = parts[0]
-            loop(16, lambda b: start(*r2_args(b)))
+            loop(16, lambda i: start(*r2_args((z + 8 + jnp.where(i % 2 == 0, 16 - i // 2, (i + 1) // 2)) % 16)))
 
     def whole_sum(what):
         @when(owns & (c == what))
@@ -410,7 +422,7 @@
             while len(parts) > 1:
                 parts = [parts[i] + parts[i + 1] for i in range(0, len(parts), 2)]
             mine[1] = parts[0] * (1.0 / CELLS)
-            loop(32, lambda n: start(*r3_args(n)))
+            loop(32, lambda n: start(*r3_args(far_group(n // 4) * 4 + n % 4)))
 
     meet_sums(0)
     plane_sum(0)
@@ -426,9 +438,17 @@
 
     @when(meets)
     def _():
-        for s in range(8):
-            rot[:, s, :] = jnp.dot(inverse, every[0, :, s, :], precision=HI, preferred_element_type=F32)
-        loop(8, lambda b: start(*o_args(b)))
+        inv[...] = inverse
+
+        def rotate(i):
+            half = (o // 4 + 1 + i) % 2
+            rows = pl.ds(pl.multiple_of(half * 48, 8), 48)
+            part = inv[rows, :]
+            for s in range(8):
+                rot[rows, s, :] = jnp.dot(part, every[0, :, s, :], precision=HI, preferred_element_type=F32)
+            loop(4, lambda n: start(*o_args(half * 4 + (o % 4 + jnp.where(n == 0, 2, n + n // 3 - 1)) % 4)))
+
+        loop(2, rotate)
 
     whole_sum(1)
 
@@ -500,6 +520,7 @@
             pltpu.VMEM((2, 12, 8, 128), F32),
             pltpu.VMEM((NORB, 8, 128), F32),
             pltpu.VMEM((NORB, NORB), F32),
+            pltpu.VMEM((NORB, NORB), F32),
             dma((12,)), dma, dma((12,)), dma((4,)), dma((32,)), dma((6,)), dma((2,)), dma((2,)),
             dma((2, 32)), dma((2,)), pltpu.SemaphoreType.REGULAR,
             dma((2, 12)), dma, dma((16,)), dma, dma((32,)), dma((2,)), dma((8,)), dma, dma,

time: 115 us -> 114 us (level)
    pallas_call x1, Pallas kernels: 112 us -> 111 us  [local(): pl.pallas_call(kernel, out_shape=(jax.ShapeDtypeStruct(orbitals.shape, F3...]
where the time goes in v6:
time: 114 us
  Pallas kernels  111 us (97%)
  local copies, waits for them, and re-layouts  2.33 us (2%)
    pallas_call x1, Pallas kernels, local(): pl.pallas_call(kernel, out_shape=(jax.ShapeDtypeStruct(orbitals.shape, F3...  111 us
    unnamed x4, local copies, waits for them, and re-layouts  2.33 us

profile of v6, /device:TPU:1, one launch (start us, length us, event | category | flops | bytes accessed | tf_op | source)
XLA Modules:
  0.0 114.1 jit_solution(8777311036464049480)
XLA Ops:
  0.6 111.1 %filter_and_rotate.1 = (f32[12,1,6,8,128]{4,3,2,1,0:T(8,128)}, f32[96,96]{1,0:T(8,128)}) custom-call(f32[12,1,6,8,128]{4,3,2,1,0:T(8,128)} %orb_ref.1, f32[1,6,8,128]{3,2,1,0:T(8,128)} %pot_ref.1), custom_call_target="tpu_custom_call" | custom-call | tf_op jit(solution)/shard_map/filter_and_rotate/pallas_call | solution.py:501
  111.7 0.0 copy-start
  111.7 1.7 %copy.6 = f32[12,1,6,8,128]{4,3,2,1,0:T(8,128)} copy(f32[12,1,6,8,128]{4,3,2,1,0:T(8,128)} %get-tuple-element.4) | data formatting | bytes 589824
  113.4 0.0 copy-done
  113.4 0.6 copy.7
Async XLA Ops:
  111.7 1.7 %copy-start = (f32[96,96]{1,0:T(8,128)S(1)}, f32[96,96]{1,0:T(8,128)}, u32[]{:S(2)}) copy-start(f32[96,96]{1,0:T(8,128)} %get-tuple-element.5) | copy-start | bytes 110596

commit v7 on v6

--- a/solution.py
+++ b/solution.py
@@ -73,6 +73,14 @@
 
 def over_rows(tile, r):
     return jnp.broadcast_to(tile[r : r + 1, :], (8, 128))
+
+
+def split(every, what):
+    x = jnp.concatenate([every[what, :, s, :] for s in range(8)], axis=1)
+    high = x.astype(jnp.bfloat16)
+    rest = x - high.astype(F32)
+    middle = rest.astype(jnp.bfloat16)
+    return high, middle, (rest - middle.astype(F32)).astype(jnp.bfloat16)
 
 
 def inverse_factor(matrix):
@@ -393,12 +401,13 @@
         @when(meets)
         def _():
             landed(every.at[what], m_recv.at[what])
-            acc = jnp.zeros((NORB, NORB), F32)
-            for s in range(8):
-                acc = acc + lax.dot_general(
-                    every[0, :, s, :], every[what, :, s, :], (((1,), (1,)), ((), ())),
-                    precision=HI, preferred_element_type=F32,
-                )
+            left_parts, right_parts = split(every, 0), split(every, what)
+            pairs = ((0, 0), (0, 1), (1, 0), (1, 1), (0, 2), (2, 0))
+            acc = lax.dot_general(
+                jnp.concatenate([left_parts[a] for a, _ in pairs], axis=1),
+                jnp.concatenate([right_parts[b] for _, b in pairs], axis=1),
+                (((1,), (1,)), ((), ())), preferred_element_type=F32,
+            )
             for m in range(12):
                 gram[what, m] = jnp.zeros((8, 128), F32)
                 gram[what, m, :, 0:NORB] = acc[8 * m : 8 * m + 8, :]

time: 114 us -> 114 us (level)
  no operation moved by 1% of the time
where the time goes in v7:
time: 114 us
  Pallas kernels  111 us (97%)
  local copies, waits for them, and re-layouts  2.33 us (2%)
    pallas_call x1, Pallas kernels, local(): pl.pallas_call(kernel, out_shape=(jax.ShapeDtypeStruct(orbitals.shape, F3...  111 us
    unnamed x4, local copies, waits for them, and re-layouts  2.33 us

profile of v7, /device:TPU:1, one launch (start us, length us, event | category | flops | bytes accessed | tf_op | source)
XLA Modules:
  0.0 114.1 jit_solution(6386812036141791026)
XLA Ops:
  0.6 111.1 %filter_and_rotate.1 = (f32[12,1,6,8,128]{4,3,2,1,0:T(8,128)}, f32[96,96]{1,0:T(8,128)}) custom-call(f32[12,1,6,8,128]{4,3,2,1,0:T(8,128)} %orb_ref.1, f32[1,6,8,128]{3,2,1,0:T(8,128)} %pot_ref.1), custom_call_target="tpu_custom_call" | custom-call | tf_op jit(solution)/shard_map/filter_and_rotate/pallas_call | solution.py:510
  111.7 0.0 copy-start
  111.7 1.7 %copy.6 = f32[12,1,6,8,128]{4,3,2,1,0:T(8,128)} copy(f32[12,1,6,8,128]{4,3,2,1,0:T(8,128)} %get-tuple-element.4) | data formatting | bytes 589824
  113.4 0.0 copy-done
  113.4 0.6 copy.7
Async XLA Ops:
  111.7 1.7 %copy-start = (f32[96,96]{1,0:T(8,128)S(1)}, f32[96,96]{1,0:T(8,128)}, u32[]{:S(2)}) copy-start(f32[96,96]{1,0:T(8,128)} %get-tuple-element.5) | copy-start | bytes 110596
